TPU v7x, 128 devices: a whole 4x4x4 slice. The times are simulated.
128 devices in a mesh: side: 2 (over core), dp: 16 (over x, y), tp: 4 (over z).
Axes of the slice: x: 4, y: 4, z: 4, core: 2. Of those that a mesh axis runs over, the one named last changes fastest.
Arguments:
- hidden_in: bfloat16 [4, 1024, 4096], P(None, ('side', 'dp', 'tp')), may hold values from -6 to 6
- queries: bfloat16 [4, 1024, 4096], P(None, ('side', 'dp'), 'tp'), may hold values from -90 to 90
- new_kv: bfloat16 [4, 2, 1024, 512], P(None, None, ('side', 'dp'), 'tp'), may hold values from -5 to 5
- cache: bfloat16 [2, 1024, 128, 512], P(None, ('side', 'dp'), None, 'tp'), may hold values from -5 to 5, as said below
- lengths: int32 [1024], P(('side', 'dp')), may hold values from 2 to 124, as said below
- out_weight: bfloat16 [4096, 4096], P('tp'), may hold values from -0.375 to 0.375
- norm_gain: bfloat16 [4096], replicated, may hold values from 0.5 to 1.5
- routes: int32 [4, 1024, 8], P(None, ('side', 'dp', 'tp')), may hold values from 0 to 63, all different within a row; in each aligned block of 8 rows (0 to 7, 8 to 15, ..., all dimensions but the last counted through in order) at most 2 rows name the same one
- route_weights: float32 [4, 1024, 8], P(None, ('side', 'dp', 'tp')), may hold values from 0.1 to 1
- w_gate: bfloat16 [64, 4096, 1280], P(('dp', 'tp'), None, 'side'), may hold values from -0.09375 to 0.09375
- w_up: bfloat16 [64, 4096, 1280], P(('dp', 'tp'), None, 'side'), may hold values from -0.09375 to 0.09375
- w_down: bfloat16 [64, 1280, 4096], P(('dp', 'tp'), 'side'), may hold values from -0.15625 to 0.15625
Outputs:
- layer_out: bfloat16 [4, 1024, 4096], P(None, ('side', 'dp', 'tp'))
Inputs may be any that keep to these rules, and one draw needn't show every extreme that they name: `routes`: each row names 8 different experts. Among the 8 rows of one device in one step (aligned blocks of rows, steps then requests in order) no expert is named more than 2 times, and that bound is reached. `lengths`: the largest length is reached by some request. Entries at cache positions at or past a request's length are not used.
All inputs are finite; a program needn't handle non-finite values.
Results may differ from a plain program's by a relative error of at most 0.022.
Values may be sent and summed in bfloat16 or wider, within the bound.
No kernel may reach another device: no remote copies, remote signals or barrier semaphores. Data moves between devices by JAX's collectives and lax.ppermute only.
A program may use at most 128 MiB of HBM per device.

v0:
```python
import math

import jax
import jax.numpy as jnp
from jax import lax
from jax.sharding import PartitionSpec as P

H = 32
KVH = 4
HD = 128


EPSILON = 1e-06
NEGATIVE = -1e30


def softmax_pair(old_scores, new_scores):
    row_max = jnp.maximum(jnp.max(old_scores, axis=-1), jnp.max(new_scores, axis=-1))
    old_exp = jnp.exp(old_scores - row_max[..., None])
    new_exp = jnp.exp(new_scores - row_max[..., None])
    row_total = jnp.sum(old_exp, axis=-1) + jnp.sum(new_exp, axis=-1)
    old_probs = (old_exp / row_total[..., None]).astype(jnp.bfloat16)
    new_probs = (new_exp / row_total[..., None]).astype(jnp.bfloat16)
    return (old_probs, new_probs)


def attend(queries, new_kv, cache, lengths):
    steps, reqs = queries.shape[0], queries.shape[1]
    group = H // KVH
    context = cache.shape[2]
    scale = 1.0 / math.sqrt(HD)
    query = queries.reshape(steps, reqs, group, HD).transpose(1, 0, 2, 3)
    query = query.reshape(reqs, steps * group, HD)
    old_scores = (
        jnp.einsum("rqd,rcd->rqc", query, cache[0], preferred_element_type=jnp.float32) * scale
    )
    valid = jnp.arange(context, dtype=jnp.int32)[None, :] < lengths[:, None]
    old_scores = jnp.where(valid[:, None, :], old_scores, NEGATIVE)
    new_scores = (
        jnp.einsum("rqd,trd->rqt", query, new_kv[:, 0], preferred_element_type=jnp.float32) * scale
    )
    step_of_row = jnp.arange(steps * group, dtype=jnp.int32) // group
    causal = jnp.arange(steps, dtype=jnp.int32)[None, :] <= step_of_row[:, None]
    new_scores = jnp.where(causal[None], new_scores, NEGATIVE)
    old_probs, new_probs = softmax_pair(old_scores, new_scores)
    attended = jnp.einsum("rqc,rcd->rqd", old_probs, cache[1], preferred_element_type=jnp.float32)
    attended = attended + jnp.einsum(
        "rqt,trd->rqd", new_probs, new_kv[:, 1], preferred_element_type=jnp.float32
    )
    return attended.astype(jnp.bfloat16)


def on_device(
    hidden_in,
    queries,
    new_kv,
    cache,
    lengths,
    out_weight,
    norm_gain,
    routes,
    route_weights,
    w_gate,
    w_up,
    w_down,
):
    steps, toks, width = hidden_in.shape
    rows = steps * toks
    reqs = queries.shape[1]
    group = H // KVH
    tp = lax.axis_size("tp")
    experts = lax.axis_size("dp") * tp
    slots = 2
    me = lax.axis_index("tp")

    attended = attend(queries, new_kv, cache, lengths)
    attended = attended.reshape(tp, toks, steps, group * HD).transpose(0, 2, 1, 3)
    projected = jnp.dot(
        attended.reshape(tp * rows, group * HD), out_weight, preferred_element_type=jnp.float32
    ).reshape(tp, rows, width)
    sent = projected.astype(jnp.bfloat16)
    total = lax.dynamic_index_in_dim(projected, me, 0, keepdims=False)
    for hop in range(1, tp):
        block = lax.dynamic_index_in_dim(sent, (me + hop) % tp, 0, keepdims=False)
        total = total + lax.ppermute(
            block, "tp", [(i, (i + hop) % tp) for i in range(tp)]
        ).astype(jnp.float32)
    resid = hidden_in.reshape(rows, width).astype(jnp.float32) + total
    normed = (
        resid
        * lax.rsqrt(jnp.mean(resid * resid, axis=-1, keepdims=True) + EPSILON)
        * norm_gain.astype(jnp.float32)
    ).astype(jnp.bfloat16)

    hits = routes[:, :, :, None] == jnp.arange(experts, dtype=jnp.int32)
    member = jnp.any(hits, axis=2)
    earlier = jnp.cumsum(member.astype(jnp.int32), axis=1) - member.astype(jnp.int32)
    weight = jnp.sum(jnp.where(hits, route_weights[..., None], 0.0), axis=2)
    same_step = jnp.eye(steps, dtype=jnp.bool_)
    place = (
        member[:, :, :, None, None]
        & same_step[:, None, None, :, None]
        & (earlier[:, :, :, None, None] == jnp.arange(slots, dtype=jnp.int32))
    )
    mixer = jnp.where(place, weight[:, :, :, None, None], 0.0).reshape(rows, -1)
    place = place.reshape(rows, experts * steps * slots).astype(jnp.bfloat16)

    outgoing = jnp.einsum("tq,td->qd", place, normed, preferred_element_type=jnp.float32)
    outgoing = outgoing.astype(jnp.bfloat16).reshape(experts, steps * slots, width)
    received = lax.all_to_all(outgoing, ("dp", "tp"), 0, 0, tiled=True).reshape(-1, width)
    swap = [(0, 1), (1, 0)]
    sibling = lax.ppermute(received, "side", swap)

    def half_expert(tokens):
        gate = jnp.dot(tokens, w_gate[0], preferred_element_type=jnp.float32)
        up = jnp.dot(tokens, w_up[0], preferred_element_type=jnp.float32)
        act = (jax.nn.silu(gate) * up).astype(jnp.bfloat16)
        return jnp.dot(act, w_down[0], preferred_element_type=jnp.float32).astype(jnp.bfloat16)

    other_part = lax.ppermute(half_expert(sibling), "side", swap)
    own_part = half_expert(received)
    combined = (own_part.astype(jnp.float32) + other_part.astype(jnp.float32)).astype(jnp.bfloat16)
    returned = lax.all_to_all(
        combined.reshape(experts, steps * slots, width), ("dp", "tp"), 0, 0, tiled=True
    ).reshape(-1, width)

    high = mixer.astype(jnp.bfloat16)
    low = (mixer - high.astype(jnp.float32)).astype(jnp.bfloat16)
    mixed = jnp.dot(
        jnp.concatenate([high, low], axis=0), returned, preferred_element_type=jnp.float32
    )
    mixture = mixed[:rows] + mixed[rows:]
    return (resid + mixture).astype(jnp.bfloat16).reshape(steps, toks, width)


def solution(mesh):
    placed = (
        P(None, ("side", "dp", "tp"), None),
        P(None, ("side", "dp"), "tp"),
        P(None, None, ("side", "dp"), "tp"),
        P(None, ("side", "dp"), None, "tp"),
        P(("side", "dp")),
        P("tp", None),
        P(),
        P(None, ("side", "dp", "tp"), None),
        P(None, ("side", "dp", "tp"), None),
        P(("dp", "tp"), None, "side"),
        P(("dp", "tp"), None, "side"),
        P(("dp", "tp"), "side", None),
    )
    return jax.shard_map(
        on_device,
        mesh=mesh,
        in_specs=placed,
        out_specs=P(None, ("side", "dp", "tp"), None),
        check_vma=False,
    )
```

profile of v0, /device:TPU:0, one launch (start us, length us, event | category | flops | bytes accessed | tf_op | source)
XLA Modules:
  0.0 196.2 jit_solution(307113686630502333)
XLA Ops:
  0.0 1.1 copy.39
  1.2 0.8 fusion.66
  1.9 0.7 iota_compare_fusion.2
  2.9 2.0 fusion.67
  6.3 4.7 %fusion.69 = (bf16[4,32,4096]{2,1,0:T(8,128)(2,1)S(1)}, f32[4,32,4096]{2,1,0:T(8,128)S(1)}) fusion(bf16[1024,4096]{1,0:T(8,128)(2,1)} %param.17, bf16[4,4,8,1024]{3,1,2,0:T(4,128)(2,1)S(1)} %bitcast.124), kind=kOutput, calls=%fused_computation.97 | convolution fusion | flops 1074266112 | bytes 11796480 | tf_op jit(solution)/shard_map/dot_general | solution.py:78
  11.0 2.1 %collective-permute-start = (bf16[32,4096]{1,0:T(8,128)(2,1)S(1)}, bf16[32,4096]{1,0:T(8,128)(2,1)}, u32[]{:S(2)}, u32[]{:S(2)}) collective-permute-start(bf16[32,4096]{1,0:T(8,128)(2,1)S(1)} %get-tuple-element.7), channel_id=1, source_target_pairs={{0,1},{1,2},{2,3},{3,0},{4,5},{5,6},{6,7},{7,4},{8,9},{9,10},{10,1... | collective-permute-start | bytes 786440 | tf_op jit(solution)/shard_map/ppermute | solution.py:85
  13.1 3.6 %collective-permute-start.1 = (bf16[32,4096]{1,0:T(8,128)(2,1)S(1)}, bf16[32,4096]{1,0:T(8,128)(2,1)}, u32[]{:S(2)}, u32[]{:S(2)}) collective-permute-start(bf16[32,4096]{1,0:T(8,128)(2,1)S(1)} %get-tuple-element.9), channel_id=1, source_target_pairs={{0,2},{1,3},{2,0},{3,1},{4,6},{5,7},{6,4},{7,5},{8,10},{9,11},{10,... | collective-permute-start | bytes 786440 | tf_op jit(solution)/shard_map/ppermute | solution.py:85
  16.7 1.0 collective-permute-start.2
  19.3 2.3 %collective-permute-done = bf16[32,4096]{1,0:T(8,128)(2,1)} collective-permute-done((bf16[32,4096]{1,0:T(8,128)(2,1)S(1)}, bf16[32,4096]{1,0:T(8,128)(2,1)}, u32[]{:S(2)}, u32[]{:S(2)}) %collective-permute-start) | collective-permute-done | bytes 262176 | tf_op jit(solution)/shard_map/ppermute | solution.py:85
  21.6 6.8 %collective-permute-done.1 = bf16[32,4096]{1,0:T(8,128)(2,1)} collective-permute-done((bf16[32,4096]{1,0:T(8,128)(2,1)S(1)}, bf16[32,4096]{1,0:T(8,128)(2,1)}, u32[]{:S(2)}, u32[]{:S(2)}) %collective-permute-start.1) | collective-permute-done | bytes 262176 | tf_op jit(solution)/shard_map/ppermute | solution.py:85
  28.4 1.5 multiply_reduce_fusion
  29.9 1.3 fusion.2
  31.2 61.8 %all_to_all.10 = bf16[64,8,4096]{2,1,0:T(8,128)(2,1)S(1)} all-to-all(bf16[64,8,4096]{2,1,0:T(8,128)(2,1)S(1)} %fusion.2), channel_id=1, replica_groups=mesh['side'=2,'dp'=16,'tp'=4] {'dp','tp'}, dimensions={0} | all-to-all | bytes 8388608 | tf_op jit(solution)/shard_map/all_to_all | solution.py:110
  93.0 7.2 %collective-permute-done.3 = bf16[512,4096]{1,0:T(8,128)(2,1)S(1)} collective-permute-done((bf16[512,4096]{1,0:T(8,128)(2,1)S(1)}, bf16[512,4096]{1,0:T(8,128)(2,1)S(1)}, u32[]{:S(2)}, u32[]{:S(2)}) %collective-permute-start.3) | collective-permute-done | bytes 4194336 | tf_op jit(solution)/shard_map/ppermute | solution.py:112
  100.2 3.4 %fusion.5 = f32[512,640]{1,0:T(8,128)S(1)} fusion(bf16[512,4096]{1,0:T(8,128)(2,1)S(1)} %collective-permute-done.3, bf16[1,4096,640]{2,1,0:T(8,128)(2,1)S(1)} %bitcast.133), kind=kOutput, calls=%fused_computation.9 | convolution fusion | flops 2684354560 | bytes 10747904 | tf_op jit(solution)/shard_map/dot_general | solution.py:116
  103.7 3.5 %fusion.9 = f32[512,640]{1,0:T(8,128)S(1)} fusion(bf16[512,4096]{1,0:T(8,128)(2,1)S(1)} %collective-permute-done.3, bf16[1,4096,640]{2,1,0:T(8,128)(2,1)S(1)} %bitcast.129), kind=kOutput, calls=%fused_computation.13 | convolution fusion | flops 2684354560 | bytes 10747904 | tf_op jit(solution)/shard_map/dot_general | solution.py:115
  107.2 3.7 %convolution_convert_fusion.1 = bf16[512,4096]{1,0:T(8,128)(2,1)S(1)} fusion(bf16[1,640,4096]{2,1,0:T(8,128)(2,1)S(1)} %bitcast.131, f32[512,640]{1,0:T(8,128)S(1)} %fusion.5, f32[512,640]{1,0:T(8,128)S(1)} %fusion.9), kind=kOutput, calls=%fused_computation.4 | convolution fusion | flops 2688417792 | bytes 12058624 | tf_op jit(solution)/shard_map/dot_general | solution.py:118
  111.3 3.4 %fusion.11 = f32[512,640]{1,0:T(8,128)S(1)} fusion(bf16[1,4096,640]{2,1,0:T(8,128)(2,1)S(1)} %bitcast.129, bf16[64,8,4096]{2,1,0:T(8,128)(2,1)S(1)} %all_to_all.10), kind=kOutput, calls=%fused_computation.15 | convolution fusion | flops 2684354560 | bytes 10747904 | tf_op jit(solution)/shard_map/dot_general | solution.py:115
  114.8 3.7 %collective-permute-done.4 = bf16[512,4096]{1,0:T(8,128)(2,1)} collective-permute-done((bf16[512,4096]{1,0:T(8,128)(2,1)S(1)}, bf16[512,4096]{1,0:T(8,128)(2,1)}, u32[]{:S(2)}, u32[]{:S(2)}) %collective-permute-start.4) | collective-permute-done | bytes 4194336 | tf_op jit(solution)/shard_map/ppermute | solution.py:120
  118.5 13.4 %fusion.15 = bf16[64,8,4096]{2,1,0:T(8,128)(2,1)} fusion(bf16[512,4096]{1,0:T(8,128)(2,1)} %collective-permute-done.4, bf16[1,640,4096]{2,1,0:T(8,128)(2,1)} %param.23, bf16[1,4096,640]{2,1,0:T(8,128)(2,1)} %param.22, f32[512,640]{1,0:T(8,128)S(1)} %fusion.11, bf16[64,8,4096]{2,1,0:T(8,128)(2,1)} %copy-done), kind=kOutput, calls=%fused_computation.17 | convolution fusion | flops 5381160960 | bytes 24379392 | tf_op jit(solution)/shard_map/dot_general | solution.py:118
  131.9 6.0 %all-to-all-start.1 = ((bf16[64,8,4096]{2,1,0:T(8,128)(2,1)}), bf16[64,8,4096]{2,1,0:T(8,128)(2,1)}, u32[]{:S(2)}, u32[]{:S(2)}) async-start(bf16[64,8,4096]{2,1,0:T(8,128)(2,1)} %fusion.15), calls=%async_computation.1 | async-start | bytes 8388608 | tf_op jit(solution)/shard_map/all_to_all | solution.py:123
  139.1 53.2 %all-to-all-done.1 = bf16[64,8,4096]{2,1,0:T(8,128)(2,1)} async-done(((bf16[64,8,4096]{2,1,0:T(8,128)(2,1)}), bf16[64,8,4096]{2,1,0:T(8,128)(2,1)}, u32[]{:S(2)}, u32[]{:S(2)}) %all-to-all-start.1) | async-done | bytes 4194336 | tf_op jit(solution)/shard_map/all_to_all | solution.py:123
  192.3 3.0 %fusion.18 = f32[64,4096]{1,0:T(8,128)S(1)} fusion(bf16[64,8,4096]{2,1,0:T(8,128)(2,1)} %all-to-all-done.1, bf16[32,512]{1,0:T(8,128)(2,1)S(1)} %subtract_convert_fusion, bf16[32,512]{1,0:T(8,128)(2,1)S(1)} %select_convert_fusion), kind=kOutput, calls=%fused_computation.18 | convolution fusion | flops 268566528 | bytes 5308416 | tf_op jit(solution)/shard_map/dot_general | solution.py:129
  195.4 0.8 fusion.41
  (60 shorter events, 4.7 us)
Async XLA Ops:
  0.0 5.7 %copy-start.4 = (bf16[2,32,128,128]{3,2,1,0:T(8,128)(2,1)S(1)}, bf16[2,32,128,128]{3,2,1,0:T(8,128)(2,1)}, u32[]{:S(2)}) copy-start(bf16[2,32,128,128]{3,2,1,0:T(8,128)(2,1)} %param.15) | copy-start | bytes 6291460
  6.2 11.5 %copy-start.1 = (s32[4,8,8]{2,1,0:T(8,128)S(1)}, s32[4,8,8]{2,1,0:T(8,128)}, u32[]{:S(2)}) copy-start(s32[4,8,8]{2,1,0:T(8,128)} %param.19) | copy-start | bytes 3076
  6.3 13.0 %copy-start.3 = (bf16[4096]{0:T(1024)(128)(2,1)S(1)}, bf16[4096]{0:T(1024)(128)(2,1)}, u32[]{:S(2)}) copy-start(bf16[4096]{0:T(1024)(128)(2,1)} %param.18) | copy-start | bytes 24580
  11.0 10.6 %collective-permute-start = (bf16[32,4096]{1,0:T(8,128)(2,1)S(1)}, bf16[32,4096]{1,0:T(8,128)(2,1)}, u32[]{:S(2)}, u32[]{:S(2)}) collective-permute-start(bf16[32,4096]{1,0:T(8,128)(2,1)S(1)} %get-tuple-element.7), channel_id=1, source_target_pairs={{0,1},{1,2},{2,3},{3,0},{4,5},{5,6},{6,7},{7,4},{8,9},{9,10},{10,1... | collective-permute-start | bytes 786440 | tf_op jit(solution)/shard_map/ppermute | solution.py:85
  13.1 15.3 %collective-permute-start.1 = (bf16[32,4096]{1,0:T(8,128)(2,1)S(1)}, bf16[32,4096]{1,0:T(8,128)(2,1)}, u32[]{:S(2)}, u32[]{:S(2)}) collective-permute-start(bf16[32,4096]{1,0:T(8,128)(2,1)S(1)} %get-tuple-element.9), channel_id=1, source_target_pairs={{0,2},{1,3},{2,0},{3,1},{4,6},{5,7},{6,4},{7,5},{8,10},{9,11},{10,... | collective-permute-start | bytes 786440 | tf_op jit(solution)/shard_map/ppermute | solution.py:85
  16.7 11.7 %collective-permute-start.2 = (bf16[32,4096]{1,0:T(8,128)(2,1)S(1)}, bf16[32,4096]{1,0:T(8,128)(2,1)}, u32[]{:S(2)}, u32[]{:S(2)}) collective-permute-start(bf16[32,4096]{1,0:T(8,128)(2,1)S(1)} %get-tuple-element.8), channel_id=1, source_target_pairs={{0,3},{1,0},{2,1},{3,2},{4,7},{5,4},{6,5},{7,6},{8,11},{9,8},{10,9... | collective-permute-start | bytes 786440 | tf_op jit(solution)/shard_map/ppermute | solution.py:85
  29.9 70.3 %slice-start.4 = ((s8[5242880]{0:T(1024)(128)(4,1)}), s8[4194304]{0:T(1024)(128)(4,1)S(1)}, s32[]{:S(2)}) async-start(s8[5242880]{0:T(1024)(128)(4,1)} %bitcast.132), calls=%async_computation.6 | async-start | bytes 8388608
  31.2 69.0 %slice-start.5 = ((s8[5242880]{0:T(1024)(128)(4,1)}), s8[1048576]{0:T(1024)(128)(4,1)S(1)}, s32[]{:S(2)}) async-start(s8[5242880]{0:T(1024)(128)(4,1)} %bitcast.132), calls=%async_computation.7 | async-start | bytes 2097152
  93.0 18.3 %copy-start = (bf16[64,8,4096]{2,1,0:T(8,128)(2,1)}, bf16[64,8,4096]{2,1,0:T(8,128)(2,1)S(1)}, u32[]{:S(2)}) copy-start(bf16[64,8,4096]{2,1,0:T(8,128)(2,1)S(1)} %all_to_all.10) | copy-start | bytes 12582916
  93.0 10.6 %slice-start = ((s8[5242880]{0:T(1024)(128)(4,1)}), s8[4194304]{0:T(1024)(128)(4,1)S(1)}, s32[]{:S(2)}) async-start(s8[5242880]{0:T(1024)(128)(4,1)} %bitcast.128), calls=%async_computation.2 | async-start | bytes 8388608
  93.0 10.6 %slice-start.1 = ((s8[5242880]{0:T(1024)(128)(4,1)}), s8[1048576]{0:T(1024)(128)(4,1)S(1)}, s32[]{:S(2)}) async-start(s8[5242880]{0:T(1024)(128)(4,1)} %bitcast.128), calls=%async_computation.3 | async-start | bytes 2097152
  93.0 7.2 %collective-permute-start.3 = (bf16[512,4096]{1,0:T(8,128)(2,1)S(1)}, bf16[512,4096]{1,0:T(8,128)(2,1)S(1)}, u32[]{:S(2)}, u32[]{:S(2)}) collective-permute-start(bf16[512,4096]{1,0:T(8,128)(2,1)S(1)} %bitcast.123), channel_id=1, source_target_pairs={{0,64},{64,0},{1,65},{65,1},{2,66},{66,2},{3,67},{67,3},{4,68},{68... | collective-permute-start | bytes 12582920 | tf_op jit(solution)/shard_map/ppermute | solution.py:112
  100.2 7.0 %slice-start.2 = ((s8[5242880]{0:T(1024)(128)(4,1)}), s8[4194304]{0:T(1024)(128)(4,1)S(1)}, s32[]{:S(2)}) async-start(s8[5242880]{0:T(1024)(128)(4,1)} %bitcast.130), calls=%async_computation.4 | async-start | bytes 8388608
  103.7 3.5 %slice-start.3 = ((s8[5242880]{0:T(1024)(128)(4,1)}), s8[1048576]{0:T(1024)(128)(4,1)S(1)}, s32[]{:S(2)}) async-start(s8[5242880]{0:T(1024)(128)(4,1)} %bitcast.130), calls=%async_computation.5 | async-start | bytes 2097152
  110.9 7.6 %collective-permute-start.4 = (bf16[512,4096]{1,0:T(8,128)(2,1)S(1)}, bf16[512,4096]{1,0:T(8,128)(2,1)}, u32[]{:S(2)}, u32[]{:S(2)}) collective-permute-start(bf16[512,4096]{1,0:T(8,128)(2,1)S(1)} %convolution_convert_fusion.1), channel_id=1, source_target_pairs={{0,64},{64,0},{1,65},{65,1},{2,66},{66,2},{3,67},{67,3},{4,68},{68... | collective-permute-start | bytes 12582920 | tf_op jit(solution)/shard_map/ppermute | solution.py:120
  131.9 6.2 %copy-start.2 = (f32[4,8,8]{2,1,0:T(8,128)S(1)}, f32[4,8,8]{2,1,0:T(8,128)}, u32[]{:S(2)}) copy-start(f32[4,8,8]{2,1,0:T(8,128)} %param.20) | copy-start | bytes 3076
  131.9 60.4 %all-to-all-start.1 = ((bf16[64,8,4096]{2,1,0:T(8,128)(2,1)}), bf16[64,8,4096]{2,1,0:T(8,128)(2,1)}, u32[]{:S(2)}, u32[]{:S(2)}) async-start(bf16[64,8,4096]{2,1,0:T(8,128)(2,1)} %fusion.15), calls=%async_computation.1 | async-start | bytes 8388608 | tf_op jit(solution)/shard_map/all_to_all | solution.py:123
where the time goes:
time: 199 us; the launch traced here: 196 us
  waiting for transfers between devices  73.2 us (37%)
  blocking collectives  61.8 us (31%)
  matrix products  39.4 us (20%)
  starting transfers between devices  13.1 us (7%)
  other arithmetic  4.61 us (2%)
  local copies, waits for them, and re-layouts  3.61 us (2%)
    all_to_all x1, blocking collectives, on_device(): lax.all_to_all(outgoing, ('dp', 'tp'), 0, 0, tiled=True).reshape(-1, width)  61.8 us
    all_to_all x1, waiting for transfers between devices, on_device(): lax.all_to_all(combined.reshape(experts, steps * slots, width), ('dp', 't...  53.2 us
    dot_general x2, matrix products, half_expert(): jnp.dot(act, w_down[0], preferred_element_type=jnp.float32)  17.2 us
    ppermute x3, waiting for transfers between devices, on_device(): lax.ppermute(block, 'tp', [(i, (i + hop) % tp) for i in range(tp)])  9.12 us
    ppermute x1, waiting for transfers between devices, on_device(): sibling = lax.ppermute(received, 'side', swap)  7.15 us
    dot_general x2, matrix products, half_expert(): gate = jnp.dot(tokens, w_gate[0], preferred_element_type=jnp.float32)  6.88 us
    ppermute x3, starting transfers between devices, on_device(): lax.ppermute(block, 'tp', [(i, (i + hop) % tp) for i in range(tp)])  6.66 us
    all_to_all x1, starting transfers between devices, on_device(): lax.all_to_all(combined.reshape(experts, steps * slots, width), ('dp', 't...  6.04 us
  transfers between devices with their start and end apart: 6, of which 5 were waited for; matrix products, arithmetic and copies ran while one was open for 3% of the time, Pallas kernels for 0%

commit v1 on v0

--- a/solution.py
+++ b/solution.py
@@ -3,6 +3,8 @@
 import jax
 import jax.numpy as jnp
 from jax import lax
+from jax.experimental import pallas as pl
+from jax.experimental.pallas import tpu as pltpu
 from jax.sharding import PartitionSpec as P
 
 H = 32
@@ -48,6 +50,47 @@
         "rqt,trd->rqd", new_probs, new_kv[:, 1], preferred_element_type=jnp.float32
     )
     return attended.astype(jnp.bfloat16)
+
+
+def ffn_kernel(x_ref, gate_ref, up_ref, down_ref, *rest):
+    x = x_ref[...]
+    gate = jnp.dot(x, gate_ref[...], preferred_element_type=jnp.float32)
+    up = jnp.dot(x, up_ref[...], preferred_element_type=jnp.float32)
+    act = (gate / (1.0 + jnp.exp(-gate)) * up).astype(jnp.bfloat16)
+    part = jnp.dot(act, down_ref[...], preferred_element_type=jnp.float32).astype(jnp.bfloat16)
+    if len(rest) == 2:
+        part = (part.astype(jnp.float32) + rest[0][...].astype(jnp.float32)).astype(jnp.bfloat16)
+    rest[-1][...] = part
+
+
+BLOCK = 256
+
+
+def half_expert(tokens, first, count, w_gate, w_up, w_down, other=None, out_rows=None):
+    width = tokens.shape[1]
+    start = first // BLOCK
+    shift = 0 if out_rows is None else start
+    row = pl.BlockSpec((BLOCK, width), lambda i: (i + start, 0))
+    plain = pl.BlockSpec((BLOCK, width), lambda i: (i, 0))
+    whole = pl.BlockSpec(memory_space=pltpu.VMEM)
+    args = [tokens, w_gate, w_up, w_down]
+    specs = [row, whole, whole, whole]
+    if other is not None:
+        args.append(other)
+        specs.append(plain)
+    macs = count * width * w_gate.shape[1] * 3
+    return pl.pallas_call(
+        ffn_kernel,
+        grid=(count // BLOCK,),
+        in_specs=specs,
+        out_specs=pl.BlockSpec((BLOCK, width), lambda i: (i + shift, 0)),
+        out_shape=jax.ShapeDtypeStruct((out_rows or count, width), jnp.bfloat16),
+        compiler_params=pltpu.CompilerParams(vmem_limit_bytes=16 * 1024 * 1024),
+        cost_estimate=pl.CostEstimate(
+            flops=2 * macs, bytes_accessed=4 * count * width, transcendentals=count * 640
+        ),
+        name="half_expert",
+    )(*args)
 
 
 def on_device(
@@ -109,17 +152,18 @@
     outgoing = outgoing.astype(jnp.bfloat16).reshape(experts, steps * slots, width)
     received = lax.all_to_all(outgoing, ("dp", "tp"), 0, 0, tiled=True).reshape(-1, width)
     swap = [(0, 1), (1, 0)]
-    sibling = lax.ppermute(received, "side", swap)
-
-    def half_expert(tokens):
-        gate = jnp.dot(tokens, w_gate[0], preferred_element_type=jnp.float32)
-        up = jnp.dot(tokens, w_up[0], preferred_element_type=jnp.float32)
-        act = (jax.nn.silu(gate) * up).astype(jnp.bfloat16)
-        return jnp.dot(act, w_down[0], preferred_element_type=jnp.float32).astype(jnp.bfloat16)
-
-    other_part = lax.ppermute(half_expert(sibling), "side", swap)
-    own_part = half_expert(received)
-    combined = (own_part.astype(jnp.float32) + other_part.astype(jnp.float32)).astype(jnp.bfloat16)
+    total_rows = received.shape[0]
+    half = total_rows // 2
+    weights = (w_gate[0], w_up[0], w_down[0])
+    sibling_back = lax.ppermute(received[half:], "side", swap)
+    sibling_front = lax.ppermute(received[:half], "side", swap)
+    own_front = half_expert(received, 0, half, *weights)
+    own_front, sibling_back = lax.optimization_barrier((own_front, sibling_back))
+    other_back = lax.ppermute(half_expert(sibling_back, 0, half, *weights), "side", swap)
+    other_front = lax.ppermute(half_expert(sibling_front, 0, half, *weights), "side", swap)
+    combined = half_expert(received, half, half, *weights, other=other_back, out_rows=total_rows)
+    front = own_front.astype(jnp.float32) + other_front.astype(jnp.float32)
+    combined = lax.dynamic_update_slice(combined, front.astype(jnp.bfloat16), (0, 0))
     returned = lax.all_to_all(
         combined.reshape(experts, steps * slots, width), ("dp", "tp"), 0, 0, tiled=True
     ).reshape(-1, width)

time: 199 us -> 185 us (0.930)
  the two profiles are of different devices: /device:TPU:0 before, /device:TPU:82 now
where the time goes in v1:
time: 185 us
  waiting for transfers between devices  65.8 us (36%)
  blocking collectives  57.2 us (31%)
  Pallas kernels  20.9 us (11%)
  starting transfers between devices  17 us (9%)
  matrix products  12 us (6%)
  local copies, waits for them, and re-layouts  6.03 us (3%)
  other arithmetic  5.53 us (3%)
    all_to_all x1, waiting for transfers between devices, on_device(): lax.all_to_all(combined.reshape(experts, steps * slots, width), ('dp', 't...  57.4 us
    all_to_all x1, blocking collectives, on_device(): lax.all_to_all(outgoing, ('dp', 'tp'), 0, 0, tiled=True).reshape(-1, width)  57.2 us
    pallas_call x4, Pallas kernels, half_expert(): pl.pallas_call(ffn_kernel, grid=(count // BLOCK,), in_specs=specs, out_sp...  20.9 us
    all_to_all x1, starting transfers between devices, on_device(): lax.all_to_all(combined.reshape(experts, steps * slots, width), ('dp', 't...  11.7 us
    ppermute x3, waiting for transfers between devices, on_device(): lax.ppermute(block, 'tp', [(i, (i + hop) % tp) for i in range(tp)])  8.39 us
    dot_general x1, matrix products, on_device(): jnp.dot(attended.reshape(tp * rows, group * HD), out_weight, preferred_el...  4.69 us
    ppermute x3, starting transfers between devices, on_device(): lax.ppermute(block, 'tp', [(i, (i + hop) % tp) for i in range(tp)])  3.84 us
  transfers between devices with their start and end apart: 8, of which 2 were waited for; matrix products, arithmetic and copies ran while one was open for 1% of the time, Pallas kernels for 11%

profile of v1, /device:TPU:82, one launch (start us, length us, event | category | flops | bytes accessed | tf_op | source)
XLA Modules:
  0.0 184.7 jit_solution(17443656929806037510)
XLA Ops:
  0.0 0.9 iota_compare_fusion.2
  0.9 0.8 fusion.38
  1.7 1.0 copy.39
  2.9 2.0 %fusion.39 = (f32[32,32]{1,0:T(8,128)S(1)}, f32[32,32,128]{2,1,0:T(8,128)S(1)}) fusion(bf16[2,32,128,128]{3,2,1,0:T(8,128)(2,1)} %param.15, pred[32,128]{1,0:T(8,128)(4,1)S(1)} %iota_compare_fusion.2, bf16[4,32,8,128]{3,2,1,0:T(8,128)(2,1)S(1)} %bitcast.121), kind=kOutput, calls=%fused_computation.77 | convolution fusion | flops 33946624 | bytes 1843200 | tf_op jit(solution)/shard_map/rqd,rcd->rqc/dot_general | solution.py:37
  6.3 4.7 %fusion.41 = (bf16[4,32,4096]{2,1,0:T(8,128)(2,1)S(1)}, f32[4,32,4096]{2,1,0:T(8,128)S(1)}) fusion(bf16[1024,4096]{1,0:T(8,128)(2,1)} %param.17, bf16[4,4,8,1024]{3,1,2,0:T(4,128)(2,1)S(1)} %bitcast.118), kind=kOutput, calls=%fused_computation.79 | convolution fusion | flops 1074266112 | bytes 11796480 | tf_op jit(solution)/shard_map/dot_general | solution.py:121
  11.0 1.7 collective-permute-start
  13.1 1.7 collective-permute-start.1
  15.6 0.5 broadcast_and_fusion
  16.5 8.4 %collective-permute-done = bf16[32,4096]{1,0:T(8,128)(2,1)} collective-permute-done((bf16[32,4096]{1,0:T(8,128)(2,1)S(1)}, bf16[32,4096]{1,0:T(8,128)(2,1)}, u32[]{:S(2)}, u32[]{:S(2)}) %collective-permute-start) | collective-permute-done | bytes 262176 | tf_op jit(solution)/shard_map/ppermute | solution.py:128
  24.9 1.5 multiply_reduce_fusion
  26.4 1.3 fusion.2
  27.7 57.2 %all_to_all.10 = bf16[64,8,4096]{2,1,0:T(8,128)(2,1)S(1)} all-to-all(bf16[64,8,4096]{2,1,0:T(8,128)(2,1)S(1)} %fusion.2), channel_id=1, replica_groups=mesh['side'=2,'dp'=16,'tp'=4] {'dp','tp'}, dimensions={0} | all-to-all | bytes 8388608 | tf_op jit(solution)/shard_map/all_to_all | solution.py:153
  85.5 0.5 collective-permute-start.5
  86.1 5.2 %half_expert.4 = bf16[256,4096]{1,0:T(8,128)(2,1)S(1)} custom-call(bf16[512,4096]{1,0:T(8,128)(2,1)S(1)} %bitcast.115, bf16[4096,640]{1,0:T(8,128)(2,1)S(1)} %bitcast.99, bf16[4096,640]{1,0:T(8,128)(2,1)S(1)} %bitcast.105, bf16[640,4096]{1,0:T(8,128)(2,1)S(1)} %bitcast.111), custom_call_target="tpu_custom_call" | custom-call | flops 4026531840 | bytes 4194304 | tf_op jit(solution)/shard_map/half_expert/pallas_call | solution.py:82
  91.3 5.2 %half_expert.5 = bf16[256,4096]{1,0:T(8,128)(2,1)S(1)} custom-call(bf16[256,4096]{1,0:T(8,128)(2,1)S(1)} %collective-permute-done.3.x_ref, bf16[4096,640]{1,0:T(8,128)(2,1)S(1)} %bitcast.100, bf16[4096,640]{1,0:T(8,128)(2,1)S(1)} %bitcast.106, bf16[640,4096]{1,0:T(8,128)(2,1)S(1)} %bitcast.112), custom_call_target="tpu_custom_call" | custom-call | flops 4026531840 | bytes 4194304 | tf_op jit(solution)/shard_map/half_expert/pallas_call | solution.py:82
  96.5 0.5 collective-permute-start.4
  97.0 5.2 %half_expert.7 = bf16[256,4096]{1,0:T(8,128)(2,1)S(1)} custom-call(bf16[256,4096]{1,0:T(8,128)(2,1)S(1)} %collective-permute-done.5.x_ref, bf16[4096,640]{1,0:T(8,128)(2,1)S(1)} %bitcast.101, bf16[4096,640]{1,0:T(8,128)(2,1)S(1)} %bitcast.107, bf16[640,4096]{1,0:T(8,128)(2,1)S(1)} %bitcast.113), custom_call_target="tpu_custom_call" | custom-call | flops 4026531840 | bytes 4194304 | tf_op jit(solution)/shard_map/half_expert/pallas_call | solution.py:82
  102.7 5.2 %half_expert.6 = bf16[512,4096]{1,0:T(8,128)(2,1)S(1)} custom-call(bf16[512,4096]{1,0:T(8,128)(2,1)S(1)} %bitcast.116, bf16[4096,640]{1,0:T(8,128)(2,1)S(1)} %bitcast.102, bf16[4096,640]{1,0:T(8,128)(2,1)S(1)} %bitcast.108, bf16[640,4096]{1,0:T(8,128)(2,1)S(1)} %bitcast.114, bf16[256,4096]{1,0:T(8,128)(2,1)S(1)} %collective-permute-done.4.rest_0_), custom_call_target="tpu_custom_call" | custom-call | flops 4026531840 | bytes 4194304 | tf_op jit(solution)/shard_map/half_expert/pallas_call | solution.py:82
  107.9 0.8 fusion.5
  108.7 2.0 %copy-done = bf16[512,4096]{1,0:T(8,128)(2,1)} copy-done((bf16[512,4096]{1,0:T(8,128)(2,1)}, bf16[512,4096]{1,0:T(8,128)(2,1)S(1)}, u32[]{:S(2)}) %copy-start) | copy-done | bytes 4194328
  110.7 11.7 %all-to-all-start.1 = ((bf16[64,8,4096]{2,1,0:T(8,128)(2,1)}), bf16[64,8,4096]{2,1,0:T(8,128)(2,1)}, u32[]{:S(2)}, u32[]{:S(2)}) async-start(bf16[64,8,4096]{2,1,0:T(8,128)(2,1)} %bitcast.117), calls=%async_computation.1 | async-start | bytes 8388608 | tf_op jit(solution)/shard_map/all_to_all | solution.py:167
  123.5 57.4 %all-to-all-done.1 = bf16[64,8,4096]{2,1,0:T(8,128)(2,1)} async-done(((bf16[64,8,4096]{2,1,0:T(8,128)(2,1)}), bf16[64,8,4096]{2,1,0:T(8,128)(2,1)}, u32[]{:S(2)}, u32[]{:S(2)}) %all-to-all-start.1) | async-done | bytes 4194336 | tf_op jit(solution)/shard_map/all_to_all | solution.py:167
  180.9 3.0 %fusion.3 = f32[64,4096]{1,0:T(8,128)S(1)} fusion(bf16[64,8,4096]{2,1,0:T(8,128)(2,1)} %all-to-all-done.1, bf16[32,512]{1,0:T(8,128)(2,1)S(1)} %subtract_convert_fusion, bf16[32,512]{1,0:T(8,128)(2,1)S(1)} %select_convert_fusion), kind=kOutput, calls=%fused_computation.4 | convolution fusion | flops 268566528 | bytes 5308416 | tf_op jit(solution)/shard_map/dot_general | solution.py:173
  183.9 0.8 fusion.18
  (65 shorter events, 5.3 us)
Async XLA Ops:
  0.0 5.7 %copy-start.4 = (bf16[2,32,128,128]{3,2,1,0:T(8,128)(2,1)S(1)}, bf16[2,32,128,128]{3,2,1,0:T(8,128)(2,1)}, u32[]{:S(2)}) copy-start(bf16[2,32,128,128]{3,2,1,0:T(8,128)(2,1)} %param.15) | copy-start | bytes 6291460
  6.2 8.6 %copy-start.1 = (s32[4,8,8]{2,1,0:T(8,128)S(1)}, s32[4,8,8]{2,1,0:T(8,128)}, u32[]{:S(2)}) copy-start(s32[4,8,8]{2,1,0:T(8,128)} %param.19) | copy-start | bytes 3076
  6.2 9.3 %copy-start.3 = (bf16[4096]{0:T(1024)(128)(2,1)S(1)}, bf16[4096]{0:T(1024)(128)(2,1)}, u32[]{:S(2)}) copy-start(bf16[4096]{0:T(1024)(128)(2,1)} %param.18) | copy-start | bytes 24580
  11.0 13.8 %collective-permute-start = (bf16[32,4096]{1,0:T(8,128)(2,1)S(1)}, bf16[32,4096]{1,0:T(8,128)(2,1)}, u32[]{:S(2)}, u32[]{:S(2)}) collective-permute-start(bf16[32,4096]{1,0:T(8,128)(2,1)S(1)} %get-tuple-element.13), channel_id=1, source_target_pairs={{0,1},{1,2},{2,3},{3,0},{4,5},{5,6},{6,7},{7,4},{8,9},{9,10},{10,1... | collective-permute-start | bytes 786440 | tf_op jit(solution)/shard_map/ppermute | solution.py:128
  12.7 12.1 %collective-permute-start.2 = (bf16[32,4096]{1,0:T(8,128)(2,1)S(1)}, bf16[32,4096]{1,0:T(8,128)(2,1)}, u32[]{:S(2)}, u32[]{:S(2)}) collective-permute-start(bf16[32,4096]{1,0:T(8,128)(2,1)S(1)} %get-tuple-element.14), channel_id=1, source_target_pairs={{0,3},{1,0},{2,1},{3,2},{4,7},{5,4},{6,5},{7,6},{8,11},{9,8},{10,9... | collective-permute-start | bytes 786440 | tf_op jit(solution)/shard_map/ppermute | solution.py:128
  13.1 11.7 %collective-permute-start.1 = (bf16[32,4096]{1,0:T(8,128)(2,1)S(1)}, bf16[32,4096]{1,0:T(8,128)(2,1)}, u32[]{:S(2)}, u32[]{:S(2)}) collective-permute-start(bf16[32,4096]{1,0:T(8,128)(2,1)S(1)} %get-tuple-element.15), channel_id=1, source_target_pairs={{0,2},{1,3},{2,0},{3,1},{4,6},{5,7},{6,4},{7,5},{8,10},{9,11},{10,... | collective-permute-start | bytes 786440 | tf_op jit(solution)/shard_map/ppermute | solution.py:128
  26.3 59.6 %slice-start.2 = ((s8[5242880]{0:T(1024)(128)(4,1)}), s8[4194304]{0:T(1024)(128)(4,1)S(1)}, s32[]{:S(2)}) async-start(s8[5242880]{0:T(1024)(128)(4,1)} %bitcast.103), calls=%async_computation.4 | async-start | bytes 8388608
  26.4 59.6 %slice-start.4 = ((s8[5242880]{0:T(1024)(128)(4,1)}), s8[4194304]{0:T(1024)(128)(4,1)S(1)}, s32[]{:S(2)}) async-start(s8[5242880]{0:T(1024)(128)(4,1)} %bitcast.109), calls=%async_computation.6 | async-start | bytes 8388608
  27.7 58.3 %slice-start = ((s8[5242880]{0:T(1024)(128)(4,1)}), s8[4194304]{0:T(1024)(128)(4,1)S(1)}, s32[]{:S(2)}) async-start(s8[5242880]{0:T(1024)(128)(4,1)} %bitcast.97), calls=%async_computation.2 | async-start | bytes 8388608
  27.7 58.3 %slice-start.3 = ((s8[5242880]{0:T(1024)(128)(4,1)}), s8[1048576]{0:T(1024)(128)(4,1)S(1)}, s32[]{:S(2)}) async-start(s8[5242880]{0:T(1024)(128)(4,1)} %bitcast.103), calls=%async_computation.5 | async-start | bytes 2097152
  27.7 58.3 %slice-start.5 = ((s8[5242880]{0:T(1024)(128)(4,1)}), s8[1048576]{0:T(1024)(128)(4,1)S(1)}, s32[]{:S(2)}) async-start(s8[5242880]{0:T(1024)(128)(4,1)} %bitcast.109), calls=%async_computation.7 | async-start | bytes 2097152
  84.9 1.2 slice-start.1
  85.4 5.9 %collective-permute-start.3 = (bf16[256,4096]{1,0:T(8,128)(2,1)S(1)}, bf16[256,4096]{1,0:T(8,128)(2,1)S(1)}, u32[]{:S(2)}, u32[]{:S(2)}) collective-permute-start(bf16[256,4096]{1,0:T(8,128)(2,1)S(1)} %get-tuple-element.12), channel_id=1, source_target_pairs={{0,64},{64,0},{1,65},{65,1},{2,66},{66,2},{3,67},{67,3},{4,68},{68... | collective-permute-start | bytes 6291464 | tf_op jit(solution)/shard_map/ppermute | solution.py:158
  85.5 11.5 %collective-permute-start.5 = (bf16[256,4096]{1,0:T(8,128)(2,1)S(1)}, bf16[256,4096]{1,0:T(8,128)(2,1)S(1)}, u32[]{:S(2)}, u32[]{:S(2)}) collective-permute-start(bf16[256,4096]{1,0:T(8,128)(2,1)S(1)} %get-tuple-element.11), channel_id=1, source_target_pairs={{0,64},{64,0},{1,65},{65,1},{2,66},{66,2},{3,67},{67,3},{4,68},{68... | collective-permute-start | bytes 6291464 | tf_op jit(solution)/shard_map/ppermute | solution.py:159
  96.5 6.1 %collective-permute-start.4 = (bf16[256,4096]{1,0:T(8,128)(2,1)S(1)}, bf16[256,4096]{1,0:T(8,128)(2,1)S(1)}, u32[]{:S(2)}, u32[]{:S(2)}) collective-permute-start(bf16[256,4096]{1,0:T(8,128)(2,1)S(1)} %half_expert.5), channel_id=1, source_target_pairs={{0,64},{64,0},{1,65},{65,1},{2,66},{66,2},{3,67},{67,3},{4,68},{68... | collective-permute-start | bytes 6291464 | tf_op jit(solution)/shard_map/ppermute | solution.py:162
  102.3 5.7 %collective-permute-start.6 = (bf16[256,4096]{1,0:T(8,128)(2,1)S(1)}, bf16[256,4096]{1,0:T(8,128)(2,1)S(1)}, u32[]{:S(2)}, u32[]{:S(2)}) collective-permute-start(bf16[256,4096]{1,0:T(8,128)(2,1)S(1)} %half_expert.7), channel_id=1, source_target_pairs={{0,64},{64,0},{1,65},{65,1},{2,66},{66,2},{3,67},{67,3},{4,68},{68... | collective-permute-start | bytes 6291464 | tf_op jit(solution)/shard_map/ppermute | solution.py:163
  108.7 2.0 %copy-start = (bf16[512,4096]{1,0:T(8,128)(2,1)}, bf16[512,4096]{1,0:T(8,128)(2,1)S(1)}, u32[]{:S(2)}) copy-start(bf16[512,4096]{1,0:T(8,128)(2,1)S(1)} %fusion.5) | copy-start | bytes 12582916
  110.7 11.8 %copy-start.2 = (f32[4,8,8]{2,1,0:T(8,128)S(1)}, f32[4,8,8]{2,1,0:T(8,128)}, u32[]{:S(2)}) copy-start(f32[4,8,8]{2,1,0:T(8,128)} %param.20) | copy-start | bytes 3076
  110.7 70.2 %all-to-all-start.1 = ((bf16[64,8,4096]{2,1,0:T(8,128)(2,1)}), bf16[64,8,4096]{2,1,0:T(8,128)(2,1)}, u32[]{:S(2)}, u32[]{:S(2)}) async-start(bf16[64,8,4096]{2,1,0:T(8,128)(2,1)} %bitcast.117), calls=%async_computation.1 | async-start | bytes 8388608 | tf_op jit(solution)/shard_map/all_to_all | solution.py:167

commit v2 on v1

v2 whole, which is shorter than its diff:
```python
import functools
import math

import jax
import jax.numpy as jnp
from jax import lax
from jax.experimental import pallas as pl
from jax.experimental.pallas import tpu as pltpu
from jax.sharding import PartitionSpec as P

HD = 128


EPSILON = 1e-06
NEGATIVE = -1e30


def attend_project_kernel(
    me_ref, lens_ref, query_ref, new_ref, cache_hbm, weight_hbm, *rest
):
    outs, (cache_buf, weight_buf, att_buf, cache_sem, weight_sem) = rest[:-5], rest[-5:]
    parts = len(outs)
    steps, reqs = query_ref.shape[0], query_ref.shape[1]
    toks = reqs // parts
    group = query_ref.shape[2] // HD
    context = cache_buf.shape[3]
    width = weight_hbm.shape[1]
    chunk = width // parts
    rows = steps * toks
    scale = 1.0 / math.sqrt(HD)
    cache_copies = [
        pltpu.make_async_copy(
            cache_hbm.at[:, pl.ds(j * toks, toks)], cache_buf.at[j], cache_sem.at[j]
        )
        for j in range(parts)
    ]
    weight_copies = [
        pltpu.make_async_copy(
            weight_hbm.at[:, pl.ds(n * chunk, chunk)], weight_buf.at[n], weight_sem.at[n]
        )
        for n in range(parts)
    ]
    for copy in cache_copies + weight_copies:
        copy.start()
    me = me_ref[0]
    query = [
        [query_ref[s, :, g * HD : (g + 1) * HD].astype(jnp.float32) for g in range(group)]
        for s in range(steps)
    ]
    new_k = [new_ref[u, 0].astype(jnp.float32) for u in range(steps)]
    new_v = [new_ref[u, 1].astype(jnp.float32) for u in range(steps)]
    tok_old = lax.broadcasted_iota(jnp.int32, (steps * group, toks, context), 1)
    ctx_old = lax.broadcasted_iota(jnp.int32, (steps * group, toks, context), 2)
    shape_new = (steps * group, toks, steps * toks)
    tok_new = lax.broadcasted_iota(jnp.int32, shape_new, 1)
    col_new = lax.broadcasted_iota(jnp.int32, shape_new, 2)
    step_new = lax.broadcasted_iota(jnp.int32, shape_new, 0) // group
    seen = (col_new % toks == tok_new) & (col_new // toks <= step_new)
    for j in range(parts):
        part = slice(j * toks, (j + 1) * toks)
        q = jnp.concatenate([query[s][g][part] for s in range(steps) for g in range(group)], axis=0)
        q = q.astype(jnp.bfloat16)
        k_new = jnp.concatenate([x[part] for x in new_k], axis=0).astype(jnp.bfloat16)
        v_new = jnp.concatenate([x[part] for x in new_v], axis=0).astype(jnp.bfloat16)
        cache_copies[j].wait()
        keys = cache_buf[j, 0].reshape(toks * context, HD)
        contract = (((1,), (1,)), ((), ()))
        every = lax.dot_general(q, keys, contract, preferred_element_type=jnp.float32)
        every = every.reshape(steps * group, toks, toks * context)
        new = lax.dot_general(q, k_new, contract, preferred_element_type=jnp.float32)
        new = jnp.where(seen, new.reshape(shape_new) * scale, NEGATIVE)
        old = every[:, :, 0:context]
        length = jnp.full(tok_old.shape, lens_ref[j * toks], jnp.int32)
        for r in range(1, toks):
            old = jnp.where(tok_old == r, every[:, :, r * context : (r + 1) * context], old)
            length = jnp.where(tok_old == r, lens_ref[j * toks + r], length)
        old = jnp.where(ctx_old < length, old * scale, NEGATIVE)
        row_max = jnp.maximum(
            jnp.max(old, axis=-1, keepdims=True), jnp.max(new, axis=-1, keepdims=True)
        )
        old = jnp.exp(old - row_max)
        new = jnp.exp(new - row_max)
        row_total = jnp.sum(old, axis=-1, keepdims=True) + jnp.sum(new, axis=-1, keepdims=True)
        old = old / row_total
        new = (new / row_total).reshape(rows * group, steps * toks).astype(jnp.bfloat16)
        spread = jnp.concatenate(
            [jnp.where(tok_old == r, old, 0.0) for r in range(toks)], axis=-1
        )
        spread = spread.reshape(rows * group, toks * context).astype(jnp.bfloat16)
        vals = cache_buf[j, 1].reshape(toks * context, HD)
        result = jnp.dot(spread, vals, preferred_element_type=jnp.float32)
        result = result + jnp.dot(new, v_new, preferred_element_type=jnp.float32)
        result = result.reshape(steps, group, toks, HD)
        place = lax.rem(j - me + parts, parts)
        at = pl.ds(pl.multiple_of(place * rows, rows), rows)
        for g in range(group):
            att_buf[at, g * HD : (g + 1) * HD] = (
                result[:, g].reshape(rows, HD).astype(jnp.bfloat16)
            )
    for n in range(parts):
        weight_copies[n].wait()
        block = jnp.dot(att_buf[...], weight_buf[n], preferred_element_type=jnp.float32)
        for k in range(parts):
            outs[k][:, n * chunk : (n + 1) * chunk] = block[k * rows : (k + 1) * rows].astype(
                jnp.bfloat16
            )


def attend_project(queries, new_kv, cache, lengths, out_weight, me, parts):
    steps, reqs, heads_width = queries.shape
    toks = reqs // parts
    context = cache.shape[2]
    width = out_weight.shape[1]
    smem = pl.BlockSpec(memory_space=pltpu.SMEM)
    vmem = pl.BlockSpec(memory_space=pltpu.VMEM)
    hbm = pl.BlockSpec(memory_space=pl.ANY)
    rows = steps * toks
    return pl.pallas_call(
        attend_project_kernel,
        in_specs=[smem, smem, vmem, vmem, hbm, hbm],
        out_specs=[vmem] * parts,
        out_shape=[jax.ShapeDtypeStruct((rows, width), jnp.bfloat16)] * parts,
        scratch_shapes=[
            pltpu.VMEM((parts, 2, toks, context, HD), jnp.bfloat16),
            pltpu.VMEM((parts, heads_width, width // parts), jnp.bfloat16),
            pltpu.VMEM((parts * rows, heads_width), jnp.bfloat16),
            pltpu.SemaphoreType.DMA((parts,)),
            pltpu.SemaphoreType.DMA((parts,)),
        ],
        compiler_params=pltpu.CompilerParams(vmem_limit_bytes=56 * 1024 * 1024),
        name="attend_project",
    )(me.reshape(1), lengths, queries, new_kv, cache, out_weight)


def ffn_kernel(first, count, out_first, x_ref, gate_ref, up_ref, down_ref, *rest):
    out_ref = rest[-1]
    width = down_ref.shape[1]
    x = x_ref[first : first + count, :]
    gate = jnp.dot(x, gate_ref[...], preferred_element_type=jnp.float32)
    up = jnp.dot(x, up_ref[...], preferred_element_type=jnp.float32)
    act = (gate / (1.0 + jnp.exp(-gate)) * up).astype(jnp.bfloat16)
    chunk = width // 4
    for n in range(4):
        cols = slice(n * chunk, (n + 1) * chunk)
        part = jnp.dot(act, down_ref[:, cols], preferred_element_type=jnp.float32)
        part = part.astype(jnp.bfloat16)
        if len(rest) == 2:
            part = part.astype(jnp.float32) + rest[0][:, cols].astype(jnp.float32)
            part = part.astype(jnp.bfloat16)
        out_ref[out_first : out_first + count, cols] = part


def half_expert(tokens, first, count, w_gate, w_up, w_down, other=None, out_rows=None):
    width = tokens.shape[1]
    args = [tokens, w_gate, w_up, w_down] + ([] if other is None else [other])
    macs = count * width * w_gate.shape[1] * 3
    whole = pl.BlockSpec(memory_space=pltpu.VMEM)
    return pl.pallas_call(
        functools.partial(ffn_kernel, first, count, 0 if out_rows is None else first),
        in_specs=[whole] * len(args),
        out_specs=whole,
        out_shape=jax.ShapeDtypeStruct((out_rows or count, width), jnp.bfloat16),
        compiler_params=pltpu.CompilerParams(vmem_limit_bytes=16 * 1024 * 1024),
        cost_estimate=pl.CostEstimate(
            flops=2 * macs, bytes_accessed=4 * count * width, transcendentals=count * 640
        ),
        name="half_expert",
    )(*args)


def on_device(
    hidden_in,
    queries,
    new_kv,
    cache,
    lengths,
    out_weight,
    norm_gain,
    routes,
    route_weights,
    w_gate,
    w_up,
    w_down,
):
    steps, toks, width = hidden_in.shape
    rows = steps * toks
    tp = lax.axis_size("tp")
    experts = lax.axis_size("dp") * tp
    slots = 2
    me = lax.axis_index("tp")

    own, *sent = attend_project(queries, new_kv, cache, lengths, out_weight, me, tp)
    total = own.astype(jnp.float32)
    for hop in range(1, tp):
        total = total + lax.ppermute(
            sent[hop - 1], "tp", [(i, (i + hop) % tp) for i in range(tp)]
        ).astype(jnp.float32)
    resid = hidden_in.reshape(rows, width).astype(jnp.float32) + total
    normed = (
        resid
        * lax.rsqrt(jnp.mean(resid * resid, axis=-1, keepdims=True) + EPSILON)
        * norm_gain.astype(jnp.float32)
    ).astype(jnp.bfloat16)

    hits = routes[:, :, :, None] == jnp.arange(experts, dtype=jnp.int32)
    member = jnp.any(hits, axis=2)
    earlier = jnp.cumsum(member.astype(jnp.int32), axis=1) - member.astype(jnp.int32)
    weight = jnp.sum(jnp.where(hits, route_weights[..., None], 0.0), axis=2)
    same_step = jnp.eye(steps, dtype=jnp.bool_)
    place = (
        member[:, :, :, None, None]
        & same_step[:, None, None, :, None]
        & (earlier[:, :, :, None, None] == jnp.arange(slots, dtype=jnp.int32))
    )
    mixer = jnp.where(place, weight[:, :, :, None, None], 0.0).reshape(rows, -1)
    place = place.reshape(rows, experts * steps * slots).astype(jnp.bfloat16)

    outgoing = jnp.einsum("tq,td->qd", place, normed, preferred_element_type=jnp.float32)
    outgoing = outgoing.astype(jnp.bfloat16)
    high = mixer.astype(jnp.bfloat16)
    mixer = jnp.concatenate([high, (mixer - high.astype(jnp.float32)).astype(jnp.bfloat16)], axis=0)
    outgoing, mixer = lax.optimization_barrier((outgoing, mixer))
    outgoing = outgoing.reshape(experts, steps * slots, width)
    received = lax.all_to_all(outgoing, ("dp", "tp"), 0, 0, tiled=True).reshape(-1, width)
    swap = [(0, 1), (1, 0)]
    total_rows = received.shape[0]
    half = total_rows // 2
    weights = (w_gate[0], w_up[0], w_down[0])
    sibling_back = lax.ppermute(received[half:], "side", swap)
    sibling_front = lax.ppermute(received[:half], "side", swap)
    own_front = half_expert(received, 0, half, *weights)
    own_front, sibling_back = lax.optimization_barrier((own_front, sibling_back))
    other_back = lax.ppermute(half_expert(sibling_back, 0, half, *weights), "side", swap)
    other_front = lax.ppermute(half_expert(sibling_front, 0, half, *weights), "side", swap)
    combined = half_expert(received, half, half, *weights, other=other_back, out_rows=total_rows)
    front = own_front.astype(jnp.float32) + other_front.astype(jnp.float32)
    combined = lax.dynamic_update_slice(combined, front.astype(jnp.bfloat16), (0, 0))
    returned = lax.all_to_all(
        combined.reshape(experts, steps * slots, width), ("dp", "tp"), 0, 0, tiled=True
    ).reshape(-1, width)

    mixed = jnp.dot(mixer, returned, preferred_element_type=jnp.float32)
    mixture = mixed[:rows] + mixed[rows:]
    return (resid + mixture).astype(jnp.bfloat16).reshape(steps, toks, width)


def solution(mesh):
    placed = (
        P(None, ("side", "dp", "tp"), None),
        P(None, ("side", "dp"), "tp"),
        P(None, None, ("side", "dp"), "tp"),
        P(None, ("side", "dp"), None, "tp"),
        P(("side", "dp")),
        P("tp", None),
        P(),
        P(None, ("side", "dp", "tp"), None),
        P(None, ("side", "dp", "tp"), None),
        P(("dp", "tp"), None, "side"),
        P(("dp", "tp"), None, "side"),
        P(("dp", "tp"), "side", None),
    )
    return jax.shard_map(
        on_device,
        mesh=mesh,
        in_specs=placed,
        out_specs=P(None, ("side", "dp", "tp"), None),
        check_vma=False,
    )
```

time: 185 us -> 172 us (0.930)
  the two profiles are of different devices: /device:TPU:82 before, /device:TPU:0 now
where the time goes in v2:
time: 172 us
  blocking collectives  120 us (70%)
  Pallas kernels  28.3 us (16%)
  starting transfers between devices  8.14 us (5%)
  waiting for transfers between devices  8.07 us (5%)
  other arithmetic  3.01 us (2%)
  matrix products  2.17 us (1%)
  local copies, waits for them, and re-layouts  2.16 us (1%)
    all_to_all x1, blocking collectives, on_device(): lax.all_to_all(outgoing, ('dp', 'tp'), 0, 0, tiled=True).reshape(-1, width)  61.9 us
    all_to_all x1, blocking collectives, on_device(): lax.all_to_all(combined.reshape(experts, steps * slots, width), ('dp', 't...  57.9 us
    pallas_call x4, Pallas kernels, half_expert(): pl.pallas_call(functools.partial(ffn_kernel, first, count, 0 if out_rows...  20.2 us
    pallas_call x1, Pallas kernels, attend_project(): pl.pallas_call(attend_project_kernel, in_specs=[smem, smem, vmem, vmem, h...  8.1 us
    ppermute x3, waiting for transfers between devices, on_device(): lax.ppermute(sent[hop - 1], 'tp', [(i, (i + hop) % tp) for i in range(tp)])  8.06 us
    ppermute x3, starting transfers between devices, on_device(): lax.ppermute(sent[hop - 1], 'tp', [(i, (i + hop) % tp) for i in range(tp)])  6.66 us
  transfers between devices with their start and end apart: 7, of which 2 were waited for; matrix products, arithmetic and copies ran while one was open for 2% of the time, Pallas kernels for 12%

profile of v2, /device:TPU:0, one launch (start us, length us, event | category | flops | bytes accessed | tf_op | source)
XLA Modules:
  0.0 172.0 jit_solution(672036394461154319)
XLA Ops:
  0.0 8.1 %attend_project.1 = (bf16[32,4096]{1,0:T(8,128)(2,1)}, bf16[32,4096]{1,0:T(8,128)(2,1)}, bf16[32,4096]{1,0:T(8,128)(2,1)}, bf16[32,4096]{1,0:T(8,128)(2,1)}) custom-call(s32[1]{0:T(128)} %bitcast.1.me_ref, s32[32]{0:T(128)} %lens_ref.1, bf16[4,32,1024]{2,1,0:T(8,128)(2,1)} %query_ref.1, bf16[4,2,32,128]{3,2,1,0:T(8,128)(2,1)} %new_ref.1, ...), custom_call_target="tpu_custom_call" | custom-call | tf_op jit(solution)/shard_map/attend_project/pallas_call | solution.py:118
  8.1 2.1 %collective-permute-start = (bf16[32,4096]{1,0:T(8,128)(2,1)}, bf16[32,4096]{1,0:T(8,128)(2,1)S(1)}, u32[]{:S(2)}, u32[]{:S(2)}) collective-permute-start(bf16[32,4096]{1,0:T(8,128)(2,1)} %get-tuple-element.14), channel_id=1, source_target_pairs={{0,1},{1,2},{2,3},{3,0},{4,5},{5,6},{6,7},{7,4},{8,9},{9,10},{10,1... | collective-permute-start | bytes 786440 | tf_op jit(solution)/shard_map/ppermute | solution.py:195
  10.2 3.6 %collective-permute-start.1 = (bf16[32,4096]{1,0:T(8,128)(2,1)}, bf16[32,4096]{1,0:T(8,128)(2,1)S(1)}, u32[]{:S(2)}, u32[]{:S(2)}) collective-permute-start(bf16[32,4096]{1,0:T(8,128)(2,1)} %get-tuple-element.15), channel_id=1, source_target_pairs={{0,2},{1,3},{2,0},{3,1},{4,6},{5,7},{6,4},{7,5},{8,10},{9,11},{10,... | collective-permute-start | bytes 786440 | tf_op jit(solution)/shard_map/ppermute | solution.py:195
  13.8 1.0 collective-permute-start.2
  15.8 0.5 broadcast_and_fusion
  16.3 0.3 and.43
  16.9 0.5 broadcast_in_dim.39
  17.6 1.3 collective-permute-done
  18.8 6.8 %collective-permute-done.1 = bf16[32,4096]{1,0:T(8,128)(2,1)S(1)} collective-permute-done((bf16[32,4096]{1,0:T(8,128)(2,1)}, bf16[32,4096]{1,0:T(8,128)(2,1)S(1)}, u32[]{:S(2)}, u32[]{:S(2)}) %collective-permute-start.1) | collective-permute-done | bytes 262176 | tf_op jit(solution)/shard_map/ppermute | solution.py:195
  25.6 0.3 multiply_reduce_fusion
  26.0 1.3 convolution_convert_fusion
  27.3 61.9 %all_to_all.10 = bf16[64,8,4096]{2,1,0:T(8,128)(2,1)S(1)} all-to-all(bf16[64,8,4096]{2,1,0:T(8,128)(2,1)S(1)} %bitcast.47), channel_id=1, replica_groups=mesh['side'=2,'dp'=16,'tp'=4] {'dp','tp'}, dimensions={0} | all-to-all | bytes 8388608 | tf_op jit(solution)/shard_map/all_to_all | solution.py:224
  89.2 0.4 slice_bitcast_fusion
  89.7 0.5 collective-permute-start.5
  90.5 5.0 %half_expert.4 = bf16[256,4096]{1,0:T(8,128)(2,1)S(1)} custom-call(bf16[512,4096]{1,0:T(8,128)(2,1)S(1)} %bitcast.44, bf16[4096,640]{1,0:T(8,128)(2,1)S(1)} %bitcast.28, bf16[4096,640]{1,0:T(8,128)(2,1)S(1)} %bitcast.34, bf16[640,4096]{1,0:T(8,128)(2,1)S(1)} %bitcast.40), custom_call_target="tpu_custom_call" | custom-call | flops 4026531840 | bytes 4194304 | tf_op jit(solution)/shard_map/half_expert/pallas_call | solution.py:158
  95.5 5.1 %half_expert.5 = bf16[256,4096]{1,0:T(8,128)(2,1)S(1)} custom-call(bf16[256,4096]{1,0:T(8,128)(2,1)S(1)} %collective-permute-done.3.x_ref, bf16[4096,640]{1,0:T(8,128)(2,1)S(1)} %bitcast.29, bf16[4096,640]{1,0:T(8,128)(2,1)S(1)} %bitcast.35, bf16[640,4096]{1,0:T(8,128)(2,1)S(1)} %bitcast.41), custom_call_target="tpu_custom_call" | custom-call | flops 4026531840 | bytes 4194304 | tf_op jit(solution)/shard_map/half_expert/pallas_call | solution.py:158
  100.6 0.4 collective-permute-start.4
  101.0 5.0 %half_expert.7 = bf16[256,4096]{1,0:T(8,128)(2,1)S(1)} custom-call(bf16[256,4096]{1,0:T(8,128)(2,1)S(1)} %collective-permute-done.5.x_ref, bf16[4096,640]{1,0:T(8,128)(2,1)S(1)} %bitcast.30, bf16[4096,640]{1,0:T(8,128)(2,1)S(1)} %bitcast.36, bf16[640,4096]{1,0:T(8,128)(2,1)S(1)} %bitcast.42), custom_call_target="tpu_custom_call" | custom-call | flops 4026531840 | bytes 4194304 | tf_op jit(solution)/shard_map/half_expert/pallas_call | solution.py:158
  106.0 0.5 collective-permute-start.6
  106.6 5.1 %half_expert.6 = bf16[512,4096]{1,0:T(8,128)(2,1)S(1)} custom-call(bf16[512,4096]{1,0:T(8,128)(2,1)S(1)} %bitcast.45, bf16[4096,640]{1,0:T(8,128)(2,1)S(1)} %bitcast.31, bf16[4096,640]{1,0:T(8,128)(2,1)S(1)} %bitcast.37, bf16[640,4096]{1,0:T(8,128)(2,1)S(1)} %bitcast.43, bf16[256,4096]{1,0:T(8,128)(2,1)S(1)} %collective-permute-done.4.rest_0_), custom_call_target="tpu_custom_call" | custom-call | flops 4026531840 | bytes 4194304 | tf_op jit(solution)/shard_map/half_expert/pallas_call | solution.py:158
  111.7 0.8 fusion.2
  112.4 57.9 %all_to_all.11 = bf16[64,8,4096]{2,1,0:T(8,128)(2,1)S(1)} all-to-all(bf16[64,8,4096]{2,1,0:T(8,128)(2,1)S(1)} %bitcast.46), channel_id=1, replica_groups=mesh['side'=2,'dp'=16,'tp'=4] {'dp','tp'}, dimensions={0} | all-to-all | bytes 8388608 | tf_op jit(solution)/shard_map/all_to_all | solution.py:238
  170.3 0.9 fusion
  171.2 0.8 fusion.5
  (50 shorter events, 1.7 us)
Async XLA Ops:
  0.0 14.8 %copy-start.2 = (s32[4,8,8]{2,1,0:T(8,128)S(1)}, s32[4,8,8]{2,1,0:T(8,128)}, u32[]{:S(2)}) copy-start(s32[4,8,8]{2,1,0:T(8,128)} %param.19) | copy-start | bytes 3076
  0.0 15.1 %copy-start.4 = (bf16[4096]{0:T(1024)(128)(2,1)S(1)}, bf16[4096]{0:T(1024)(128)(2,1)}, u32[]{:S(2)}) copy-start(bf16[4096]{0:T(1024)(128)(2,1)} %param.18) | copy-start | bytes 24580
  0.0 15.1 %copy-start.3 = (f32[4,8,8]{2,1,0:T(8,128)S(1)}, f32[4,8,8]{2,1,0:T(8,128)}, u32[]{:S(2)}) copy-start(f32[4,8,8]{2,1,0:T(8,128)} %param.20) | copy-start | bytes 3076
  8.1 17.5 %copy-start = (bf16[4,8,4096]{2,1,0:T(8,128)(2,1)S(1)}, bf16[4,8,4096]{2,1,0:T(8,128)(2,1)}, u32[]{:S(2)}) copy-start(bf16[4,8,4096]{2,1,0:T(8,128)(2,1)} %param.12) | copy-start | bytes 786436
  8.1 17.5 %copy-start.1 = (bf16[32,4096]{1,0:T(8,128)(2,1)S(1)}, bf16[32,4096]{1,0:T(8,128)(2,1)}, u32[]{:S(2)}) copy-start(bf16[32,4096]{1,0:T(8,128)(2,1)} %get-tuple-element.13) | copy-start | bytes 786436
  8.1 10.7 %collective-permute-start = (bf16[32,4096]{1,0:T(8,128)(2,1)}, bf16[32,4096]{1,0:T(8,128)(2,1)S(1)}, u32[]{:S(2)}, u32[]{:S(2)}) collective-permute-start(bf16[32,4096]{1,0:T(8,128)(2,1)} %get-tuple-element.14), channel_id=1, source_target_pairs={{0,1},{1,2},{2,3},{3,0},{4,5},{5,6},{6,7},{7,4},{8,9},{9,10},{10,1... | collective-permute-start | bytes 786440 | tf_op jit(solution)/shard_map/ppermute | solution.py:195
  10.2 15.4 %collective-permute-start.1 = (bf16[32,4096]{1,0:T(8,128)(2,1)}, bf16[32,4096]{1,0:T(8,128)(2,1)S(1)}, u32[]{:S(2)}, u32[]{:S(2)}) collective-permute-start(bf16[32,4096]{1,0:T(8,128)(2,1)} %get-tuple-element.15), channel_id=1, source_target_pairs={{0,2},{1,3},{2,0},{3,1},{4,6},{5,7},{6,4},{7,5},{8,10},{9,11},{10,... | collective-permute-start | bytes 786440 | tf_op jit(solution)/shard_map/ppermute | solution.py:195
  13.8 11.9 %collective-permute-start.2 = (bf16[32,4096]{1,0:T(8,128)(2,1)}, bf16[32,4096]{1,0:T(8,128)(2,1)S(1)}, u32[]{:S(2)}, u32[]{:S(2)}) collective-permute-start(bf16[32,4096]{1,0:T(8,128)(2,1)} %get-tuple-element.16), channel_id=1, source_target_pairs={{0,3},{1,0},{2,1},{3,2},{4,7},{5,4},{6,5},{7,6},{8,11},{9,8},{10,9... | collective-permute-start | bytes 786440 | tf_op jit(solution)/shard_map/ppermute | solution.py:195
  26.0 64.3 %slice-start.2 = ((s8[5242880]{0:T(1024)(128)(4,1)}), s8[4194304]{0:T(1024)(128)(4,1)S(1)}, s32[]{:S(2)}) async-start(s8[5242880]{0:T(1024)(128)(4,1)} %bitcast.32), calls=%async_computation.4 | async-start | bytes 8388608
  26.0 64.3 %slice-start.4 = ((s8[5242880]{0:T(1024)(128)(4,1)}), s8[4194304]{0:T(1024)(128)(4,1)S(1)}, s32[]{:S(2)}) async-start(s8[5242880]{0:T(1024)(128)(4,1)} %bitcast.38), calls=%async_computation.6 | async-start | bytes 8388608
  27.3 62.9 %slice-start = ((s8[5242880]{0:T(1024)(128)(4,1)}), s8[4194304]{0:T(1024)(128)(4,1)S(1)}, s32[]{:S(2)}) async-start(s8[5242880]{0:T(1024)(128)(4,1)} %bitcast.26), calls=%async_computation.2 | async-start | bytes 8388608
  27.3 62.9 %slice-start.3 = ((s8[5242880]{0:T(1024)(128)(4,1)}), s8[1048576]{0:T(1024)(128)(4,1)S(1)}, s32[]{:S(2)}) async-start(s8[5242880]{0:T(1024)(128)(4,1)} %bitcast.32), calls=%async_computation.5 | async-start | bytes 2097152
  27.3 62.9 %slice-start.5 = ((s8[5242880]{0:T(1024)(128)(4,1)}), s8[1048576]{0:T(1024)(128)(4,1)S(1)}, s32[]{:S(2)}) async-start(s8[5242880]{0:T(1024)(128)(4,1)} %bitcast.38), calls=%async_computation.7 | async-start | bytes 2097152
  89.2 1.2 slice-start.1
  89.6 5.9 %collective-permute-start.3 = (bf16[256,4096]{1,0:T(8,128)(2,1)S(1)}, bf16[256,4096]{1,0:T(8,128)(2,1)S(1)}, u32[]{:S(2)}, u32[]{:S(2)}) collective-permute-start(bf16[256,4096]{1,0:T(8,128)(2,1)S(1)} %get-tuple-element.24), channel_id=1, source_target_pairs={{0,64},{64,0},{1,65},{65,1},{2,66},{66,2},{3,67},{67,3},{4,68},{68... | collective-permute-start | bytes 6291464 | tf_op jit(solution)/shard_map/ppermute | solution.py:229
  89.7 11.3 %collective-permute-start.5 = (bf16[256,4096]{1,0:T(8,128)(2,1)S(1)}, bf16[256,4096]{1,0:T(8,128)(2,1)S(1)}, u32[]{:S(2)}, u32[]{:S(2)}) collective-permute-start(bf16[256,4096]{1,0:T(8,128)(2,1)S(1)} %get-tuple-element.23), channel_id=1, source_target_pairs={{0,64},{64,0},{1,65},{65,1},{2,66},{66,2},{3,67},{67,3},{4,68},{68... | collective-permute-start | bytes 6291464 | tf_op jit(solution)/shard_map/ppermute | solution.py:230
  100.6 6.0 %collective-permute-start.4 = (bf16[256,4096]{1,0:T(8,128)(2,1)S(1)}, bf16[256,4096]{1,0:T(8,128)(2,1)S(1)}, u32[]{:S(2)}, u32[]{:S(2)}) collective-permute-start(bf16[256,4096]{1,0:T(8,128)(2,1)S(1)} %half_expert.5), channel_id=1, source_target_pairs={{0,64},{64,0},{1,65},{65,1},{2,66},{66,2},{3,67},{67,3},{4,68},{68... | collective-permute-start | bytes 6291464 | tf_op jit(solution)/shard_map/ppermute | solution.py:233
  106.0 5.6 %collective-permute-start.6 = (bf16[256,4096]{1,0:T(8,128)(2,1)S(1)}, bf16[256,4096]{1,0:T(8,128)(2,1)S(1)}, u32[]{:S(2)}, u32[]{:S(2)}) collective-permute-start(bf16[256,4096]{1,0:T(8,128)(2,1)S(1)} %half_expert.7), channel_id=1, source_target_pairs={{0,64},{64,0},{1,65},{65,1},{2,66},{66,2},{3,67},{67,3},{4,68},{68... | collective-permute-start | bytes 6291464 | tf_op jit(solution)/shard_map/ppermute | solution.py:234

commit v3 on v2

--- a/solution.py
+++ b/solution.py
@@ -18,7 +18,8 @@
 def attend_project_kernel(
     me_ref, lens_ref, query_ref, new_ref, cache_hbm, weight_hbm, *rest
 ):
-    outs, (cache_buf, weight_buf, att_buf, cache_sem, weight_sem) = rest[:-5], rest[-5:]
+    outs, rest = rest[:-7], rest[-7:]
+    cache_buf, weight_buf, att_buf, stage, cache_sem, weight_sem, out_sem = rest
     parts = len(outs)
     steps, reqs = query_ref.shape[0], query_ref.shape[1]
     toks = reqs // parts
@@ -49,43 +50,45 @@
     ]
     new_k = [new_ref[u, 0].astype(jnp.float32) for u in range(steps)]
     new_v = [new_ref[u, 1].astype(jnp.float32) for u in range(steps)]
-    tok_old = lax.broadcasted_iota(jnp.int32, (steps * group, toks, context), 1)
-    ctx_old = lax.broadcasted_iota(jnp.int32, (steps * group, toks, context), 2)
-    shape_new = (steps * group, toks, steps * toks)
-    tok_new = lax.broadcasted_iota(jnp.int32, shape_new, 1)
-    col_new = lax.broadcasted_iota(jnp.int32, shape_new, 2)
-    step_new = lax.broadcasted_iota(jnp.int32, shape_new, 0) // group
-    seen = (col_new % toks == tok_new) & (col_new // toks <= step_new)
+    lanes = (1, toks, context)
+    tok = lax.broadcasted_iota(jnp.int32, lanes, 1)
+    col = lax.broadcasted_iota(jnp.int32, lanes, 2)
+    is_tok = [tok == r for r in range(toks)]
+    same = col % toks == tok
+    seen = jnp.concatenate(
+        [
+            jnp.broadcast_to(jnp.where(same & (col // toks <= s), 0.0, NEGATIVE), (group,) + lanes[1:])
+            for s in range(steps)
+        ],
+        axis=0,
+    )
+    blank = jnp.zeros((context - steps * toks, HD), jnp.float32)
     for j in range(parts):
         part = slice(j * toks, (j + 1) * toks)
         q = jnp.concatenate([query[s][g][part] for s in range(steps) for g in range(group)], axis=0)
         q = q.astype(jnp.bfloat16)
-        k_new = jnp.concatenate([x[part] for x in new_k], axis=0).astype(jnp.bfloat16)
-        v_new = jnp.concatenate([x[part] for x in new_v], axis=0).astype(jnp.bfloat16)
+        k_new = jnp.concatenate([x[part] for x in new_k] + [blank], axis=0).astype(jnp.bfloat16)
+        v_new = jnp.concatenate([x[part] for x in new_v] + [blank], axis=0).astype(jnp.bfloat16)
         cache_copies[j].wait()
         keys = cache_buf[j, 0].reshape(toks * context, HD)
         contract = (((1,), (1,)), ((), ()))
         every = lax.dot_general(q, keys, contract, preferred_element_type=jnp.float32)
         every = every.reshape(steps * group, toks, toks * context)
         new = lax.dot_general(q, k_new, contract, preferred_element_type=jnp.float32)
-        new = jnp.where(seen, new.reshape(shape_new) * scale, NEGATIVE)
+        new = new.reshape(steps * group, toks, context) * scale + seen
         old = every[:, :, 0:context]
-        length = jnp.full(tok_old.shape, lens_ref[j * toks], jnp.int32)
+        length = jnp.full(lanes, lens_ref[j * toks], jnp.int32)
         for r in range(1, toks):
-            old = jnp.where(tok_old == r, every[:, :, r * context : (r + 1) * context], old)
-            length = jnp.where(tok_old == r, lens_ref[j * toks + r], length)
-        old = jnp.where(ctx_old < length, old * scale, NEGATIVE)
-        row_max = jnp.maximum(
-            jnp.max(old, axis=-1, keepdims=True), jnp.max(new, axis=-1, keepdims=True)
-        )
+            old = jnp.where(is_tok[r], every[:, :, r * context : (r + 1) * context], old)
+            length = jnp.where(is_tok[r], lens_ref[j * toks + r], length)
+        old = jnp.where(col < length, old * scale, NEGATIVE)
+        row_max = jnp.max(jnp.maximum(old, new), axis=-1, keepdims=True)
         old = jnp.exp(old - row_max)
         new = jnp.exp(new - row_max)
-        row_total = jnp.sum(old, axis=-1, keepdims=True) + jnp.sum(new, axis=-1, keepdims=True)
-        old = old / row_total
-        new = (new / row_total).reshape(rows * group, steps * toks).astype(jnp.bfloat16)
-        spread = jnp.concatenate(
-            [jnp.where(tok_old == r, old, 0.0) for r in range(toks)], axis=-1
-        )
+        inverse = 1.0 / jnp.sum(old + new, axis=-1, keepdims=True)
+        old = old * inverse
+        new = (new * inverse).reshape(rows * group, context).astype(jnp.bfloat16)
+        spread = jnp.concatenate([jnp.where(is_tok[r], old, 0.0) for r in range(toks)], axis=-1)
         spread = spread.reshape(rows * group, toks * context).astype(jnp.bfloat16)
         vals = cache_buf[j, 1].reshape(toks * context, HD)
         result = jnp.dot(spread, vals, preferred_element_type=jnp.float32)
@@ -97,13 +100,22 @@
             att_buf[at, g * HD : (g + 1) * HD] = (
                 result[:, g].reshape(rows, HD).astype(jnp.bfloat16)
             )
+    out_copies = []
     for n in range(parts):
         weight_copies[n].wait()
         block = jnp.dot(att_buf[...], weight_buf[n], preferred_element_type=jnp.float32)
+        cols = pl.ds(n * chunk, chunk)
         for k in range(parts):
-            outs[k][:, n * chunk : (n + 1) * chunk] = block[k * rows : (k + 1) * rows].astype(
+            stage[k, :, n * chunk : (n + 1) * chunk] = block[k * rows : (k + 1) * rows].astype(
                 jnp.bfloat16
             )
+            copy = pltpu.make_async_copy(
+                stage.at[k, :, cols], outs[k].at[:, cols], out_sem.at[k, n]
+            )
+            copy.start()
+            out_copies.append(copy)
+    for copy in out_copies:
+        copy.wait()
 
 
 def attend_project(queries, new_kv, cache, lengths, out_weight, me, parts):
@@ -118,14 +130,16 @@
     return pl.pallas_call(
         attend_project_kernel,
         in_specs=[smem, smem, vmem, vmem, hbm, hbm],
-        out_specs=[vmem] * parts,
+        out_specs=[hbm] * parts,
         out_shape=[jax.ShapeDtypeStruct((rows, width), jnp.bfloat16)] * parts,
         scratch_shapes=[
             pltpu.VMEM((parts, 2, toks, context, HD), jnp.bfloat16),
             pltpu.VMEM((parts, heads_width, width // parts), jnp.bfloat16),
             pltpu.VMEM((parts * rows, heads_width), jnp.bfloat16),
+            pltpu.VMEM((parts, rows, width), jnp.bfloat16),
             pltpu.SemaphoreType.DMA((parts,)),
             pltpu.SemaphoreType.DMA((parts,)),
+            pltpu.SemaphoreType.DMA((parts, parts)),
         ],
         compiler_params=pltpu.CompilerParams(vmem_limit_bytes=56 * 1024 * 1024),
         name="attend_project",
@@ -139,8 +153,8 @@
     gate = jnp.dot(x, gate_ref[...], preferred_element_type=jnp.float32)
     up = jnp.dot(x, up_ref[...], preferred_element_type=jnp.float32)
     act = (gate / (1.0 + jnp.exp(-gate)) * up).astype(jnp.bfloat16)
-    chunk = width // 4
-    for n in range(4):
+    chunk = width // 8
+    for n in range(8):
         cols = slice(n * chunk, (n + 1) * chunk)
         part = jnp.dot(act, down_ref[:, cols], preferred_element_type=jnp.float32)
         part = part.astype(jnp.bfloat16)
@@ -166,6 +180,28 @@
         ),
         name="half_expert",
     )(*args)
+
+
+def mix_kernel(mixer_ref, returned_ref, resid_ref, out_ref):
+    rows = resid_ref.shape[0]
+    mixed = jnp.dot(mixer_ref[...], returned_ref[...], preferred_element_type=jnp.float32)
+    out_ref[...] = (resid_ref[...] + (mixed[:rows] + mixed[rows:])).astype(jnp.bfloat16)
+
+
+def mix(mixer, returned, resid):
+    rows, width = resid.shape
+    return pl.pallas_call(
+        mix_kernel,
+        in_specs=[
+            pl.BlockSpec(memory_space=pltpu.VMEM),
+            pl.BlockSpec(memory_space=pltpu.VMEM),
+            pl.BlockSpec(memory_space=pltpu.VMEM),
+        ],
+        out_specs=pl.BlockSpec(memory_space=pltpu.VMEM),
+        out_shape=jax.ShapeDtypeStruct((rows, width), jnp.bfloat16),
+        compiler_params=pltpu.CompilerParams(vmem_limit_bytes=16 * 1024 * 1024),
+        name="mix",
+    )(mixer, returned, resid)
 
 
 def on_device(
@@ -239,9 +275,7 @@
         combined.reshape(experts, steps * slots, width), ("dp", "tp"), 0, 0, tiled=True
     ).reshape(-1, width)
 
-    mixed = jnp.dot(mixer, returned, preferred_element_type=jnp.float32)
-    mixture = mixed[:rows] + mixed[rows:]
-    return (resid + mixture).astype(jnp.bfloat16).reshape(steps, toks, width)
+    return mix(mixer, returned, resid).reshape(steps, toks, width)
 
 
 def solution(mesh):

time: 172 us -> 172 us (level)
  no operation moved by 1% of the time
where the time goes in v3:
time: 172 us
  blocking collectives  120 us (70%)
  Pallas kernels  29.7 us (17%)
  starting transfers between devices  8.14 us (5%)
  waiting for transfers between devices  8.07 us (5%)
  other arithmetic  2.22 us (1%)
  local copies, waits for them, and re-layouts  2.16 us (1%)
    all_to_all x1, blocking collectives, on_device(): lax.all_to_all(outgoing, ('dp', 'tp'), 0, 0, tiled=True).reshape(-1, width)  61.9 us
    all_to_all x1, blocking collectives, on_device(): lax.all_to_all(combined.reshape(experts, steps * slots, width), ('dp', 't...  57.9 us
    pallas_call x4, Pallas kernels, half_expert(): pl.pallas_call(functools.partial(ffn_kernel, first, count, 0 if out_rows...  20.3 us
    ppermute x3, waiting for transfers between devices, on_device(): lax.ppermute(sent[hop - 1], 'tp', [(i, (i + hop) % tp) for i in range(tp)])  8.06 us
    pallas_call x1, Pallas kernels, attend_project(): pl.pallas_call(attend_project_kernel, in_specs=[smem, smem, vmem, vmem, h...  7.88 us
    ppermute x3, starting transfers between devices, on_device(): lax.ppermute(sent[hop - 1], 'tp', [(i, (i + hop) % tp) for i in range(tp)])  6.66 us
  transfers between devices with their start and end apart: 7, of which 2 were waited for; matrix products, arithmetic and copies ran while one was open for 2% of the time, Pallas kernels for 12%

profile of v3, /device:TPU:0, one launch (start us, length us, event | category | flops | bytes accessed | tf_op | source)
XLA Modules:
  0.0 171.7 jit_solution(2806737565031135675)
XLA Ops:
  0.0 7.9 %attend_project.1 = (bf16[32,4096]{1,0:T(8,128)(2,1)}, bf16[32,4096]{1,0:T(8,128)(2,1)}, bf16[32,4096]{1,0:T(8,128)(2,1)}, bf16[32,4096]{1,0:T(8,128)(2,1)}) custom-call(s32[1]{0:T(128)} %bitcast.1.me_ref, s32[32]{0:T(128)} %lens_ref.1, bf16[4,32,1024]{2,1,0:T(8,128)(2,1)} %query_ref.1, bf16[4,2,32,128]{3,2,1,0:T(8,128)(2,1)} %new_ref.1, ...), custom_call_target="tpu_custom_call" | custom-call | tf_op jit(solution)/shard_map/attend_project/pallas_call | solution.py:130
  7.9 2.1 %collective-permute-start = (bf16[32,4096]{1,0:T(8,128)(2,1)}, bf16[32,4096]{1,0:T(8,128)(2,1)S(1)}, u32[]{:S(2)}, u32[]{:S(2)}) collective-permute-start(bf16[32,4096]{1,0:T(8,128)(2,1)} %get-tuple-element.14), channel_id=1, source_target_pairs={{0,1},{1,2},{2,3},{3,0},{4,5},{5,6},{6,7},{7,4},{8,9},{9,10},{10,1... | collective-permute-start | bytes 786440 | tf_op jit(solution)/shard_map/ppermute | solution.py:231
  10.0 3.6 %collective-permute-start.1 = (bf16[32,4096]{1,0:T(8,128)(2,1)}, bf16[32,4096]{1,0:T(8,128)(2,1)S(1)}, u32[]{:S(2)}, u32[]{:S(2)}) collective-permute-start(bf16[32,4096]{1,0:T(8,128)(2,1)} %get-tuple-element.15), channel_id=1, source_target_pairs={{0,2},{1,3},{2,0},{3,1},{4,6},{5,7},{6,4},{7,5},{8,10},{9,11},{10,... | collective-permute-start | bytes 786440 | tf_op jit(solution)/shard_map/ppermute | solution.py:231
  13.6 1.0 collective-permute-start.2
  15.4 0.2 broadcast_and_fusion.1
  15.6 0.5 broadcast_and_fusion
  16.1 0.3 and.43
  16.7 0.5 broadcast_in_dim.39
  17.4 1.3 collective-permute-done
  18.6 6.8 %collective-permute-done.1 = bf16[32,4096]{1,0:T(8,128)(2,1)S(1)} collective-permute-done((bf16[32,4096]{1,0:T(8,128)(2,1)}, bf16[32,4096]{1,0:T(8,128)(2,1)S(1)}, u32[]{:S(2)}, u32[]{:S(2)}) %collective-permute-start.1) | collective-permute-done | bytes 262176 | tf_op jit(solution)/shard_map/ppermute | solution.py:231
  25.4 0.3 multiply_reduce_fusion
  25.8 1.3 convolution_convert_fusion
  27.1 61.9 %all_to_all.10 = bf16[64,8,4096]{2,1,0:T(8,128)(2,1)S(1)} all-to-all(bf16[64,8,4096]{2,1,0:T(8,128)(2,1)S(1)} %bitcast.44), channel_id=1, replica_groups=mesh['side'=2,'dp'=16,'tp'=4] {'dp','tp'}, dimensions={0} | all-to-all | bytes 8388608 | tf_op jit(solution)/shard_map/all_to_all | solution.py:260
  89.0 0.5 slice_bitcast_fusion
  89.6 0.5 collective-permute-start.5
  90.3 5.0 %half_expert.4 = bf16[256,4096]{1,0:T(8,128)(2,1)S(1)} custom-call(bf16[512,4096]{1,0:T(8,128)(2,1)S(1)} %bitcast.40, bf16[4096,640]{1,0:T(8,128)(2,1)S(1)} %bitcast.24, bf16[4096,640]{1,0:T(8,128)(2,1)S(1)} %bitcast.30, bf16[640,4096]{1,0:T(8,128)(2,1)S(1)} %bitcast.36), custom_call_target="tpu_custom_call" | custom-call | flops 4026531840 | bytes 4194304 | tf_op jit(solution)/shard_map/half_expert/pallas_call | solution.py:172
  95.3 5.1 %half_expert.5 = bf16[256,4096]{1,0:T(8,128)(2,1)S(1)} custom-call(bf16[256,4096]{1,0:T(8,128)(2,1)S(1)} %collective-permute-done.3.x_ref, bf16[4096,640]{1,0:T(8,128)(2,1)S(1)} %bitcast.25, bf16[4096,640]{1,0:T(8,128)(2,1)S(1)} %bitcast.31, bf16[640,4096]{1,0:T(8,128)(2,1)S(1)} %bitcast.37), custom_call_target="tpu_custom_call" | custom-call | flops 4026531840 | bytes 4194304 | tf_op jit(solution)/shard_map/half_expert/pallas_call | solution.py:172
  100.4 0.5 collective-permute-start.4
  100.9 5.0 %half_expert.7 = bf16[256,4096]{1,0:T(8,128)(2,1)S(1)} custom-call(bf16[256,4096]{1,0:T(8,128)(2,1)S(1)} %collective-permute-done.5.x_ref, bf16[4096,640]{1,0:T(8,128)(2,1)S(1)} %bitcast.26, bf16[4096,640]{1,0:T(8,128)(2,1)S(1)} %bitcast.32, bf16[640,4096]{1,0:T(8,128)(2,1)S(1)} %bitcast.38), custom_call_target="tpu_custom_call" | custom-call | flops 4026531840 | bytes 4194304 | tf_op jit(solution)/shard_map/half_expert/pallas_call | solution.py:172
  105.9 0.4 collective-permute-start.6
  106.3 5.1 %half_expert.6 = bf16[512,4096]{1,0:T(8,128)(2,1)S(1)} custom-call(bf16[512,4096]{1,0:T(8,128)(2,1)S(1)} %bitcast.41, bf16[4096,640]{1,0:T(8,128)(2,1)S(1)} %bitcast.27, bf16[4096,640]{1,0:T(8,128)(2,1)S(1)} %bitcast.33, bf16[640,4096]{1,0:T(8,128)(2,1)S(1)} %bitcast.39, bf16[256,4096]{1,0:T(8,128)(2,1)S(1)} %collective-permute-done.4.rest_0_), custom_call_target="tpu_custom_call" | custom-call | flops 4026531840 | bytes 4194304 | tf_op jit(solution)/shard_map/half_expert/pallas_call | solution.py:172
  111.5 0.8 fusion
  112.3 57.9 %all_to_all.11 = bf16[64,8,4096]{2,1,0:T(8,128)(2,1)S(1)} all-to-all(bf16[64,8,4096]{2,1,0:T(8,128)(2,1)S(1)} %bitcast.42), channel_id=1, replica_groups=mesh['side'=2,'dp'=16,'tp'=4] {'dp','tp'}, dimensions={0} | all-to-all | bytes 8388608 | tf_op jit(solution)/shard_map/all_to_all | solution.py:274
  170.2 1.6 mix.1
  (49 shorter events, 1.4 us)
Async XLA Ops:
  0.0 14.6 %copy-start.2 = (s32[4,8,8]{2,1,0:T(8,128)S(1)}, s32[4,8,8]{2,1,0:T(8,128)}, u32[]{:S(2)}) copy-start(s32[4,8,8]{2,1,0:T(8,128)} %param.19) | copy-start | bytes 3076
  0.0 14.9 %copy-start.4 = (bf16[4096]{0:T(1024)(128)(2,1)S(1)}, bf16[4096]{0:T(1024)(128)(2,1)}, u32[]{:S(2)}) copy-start(bf16[4096]{0:T(1024)(128)(2,1)} %param.18) | copy-start | bytes 24580
  0.0 14.9 %copy-start.3 = (f32[4,8,8]{2,1,0:T(8,128)S(1)}, f32[4,8,8]{2,1,0:T(8,128)}, u32[]{:S(2)}) copy-start(f32[4,8,8]{2,1,0:T(8,128)} %param.20) | copy-start | bytes 3076
  7.9 17.5 %copy-start = (bf16[4,8,4096]{2,1,0:T(8,128)(2,1)S(1)}, bf16[4,8,4096]{2,1,0:T(8,128)(2,1)}, u32[]{:S(2)}) copy-start(bf16[4,8,4096]{2,1,0:T(8,128)(2,1)} %param.12) | copy-start | bytes 786436
  7.9 17.5 %copy-start.1 = (bf16[32,4096]{1,0:T(8,128)(2,1)S(1)}, bf16[32,4096]{1,0:T(8,128)(2,1)}, u32[]{:S(2)}) copy-start(bf16[32,4096]{1,0:T(8,128)(2,1)} %get-tuple-element.13) | copy-start | bytes 786436
  7.9 10.7 %collective-permute-start = (bf16[32,4096]{1,0:T(8,128)(2,1)}, bf16[32,4096]{1,0:T(8,128)(2,1)S(1)}, u32[]{:S(2)}, u32[]{:S(2)}) collective-permute-start(bf16[32,4096]{1,0:T(8,128)(2,1)} %get-tuple-element.14), channel_id=1, source_target_pairs={{0,1},{1,2},{2,3},{3,0},{4,5},{5,6},{6,7},{7,4},{8,9},{9,10},{10,1... | collective-permute-start | bytes 786440 | tf_op jit(solution)/shard_map/ppermute | solution.py:231
  10.0 15.4 %collective-permute-start.1 = (bf16[32,4096]{1,0:T(8,128)(2,1)}, bf16[32,4096]{1,0:T(8,128)(2,1)S(1)}, u32[]{:S(2)}, u32[]{:S(2)}) collective-permute-start(bf16[32,4096]{1,0:T(8,128)(2,1)} %get-tuple-element.15), channel_id=1, source_target_pairs={{0,2},{1,3},{2,0},{3,1},{4,6},{5,7},{6,4},{7,5},{8,10},{9,11},{10,... | collective-permute-start | bytes 786440 | tf_op jit(solution)/shard_map/ppermute | solution.py:231
  13.6 11.8 %collective-permute-start.2 = (bf16[32,4096]{1,0:T(8,128)(2,1)}, bf16[32,4096]{1,0:T(8,128)(2,1)S(1)}, u32[]{:S(2)}, u32[]{:S(2)}) collective-permute-start(bf16[32,4096]{1,0:T(8,128)(2,1)} %get-tuple-element.16), channel_id=1, source_target_pairs={{0,3},{1,0},{2,1},{3,2},{4,7},{5,4},{6,5},{7,6},{8,11},{9,8},{10,9... | collective-permute-start | bytes 786440 | tf_op jit(solution)/shard_map/ppermute | solution.py:231
  25.7 64.4 %slice-start.2 = ((s8[5242880]{0:T(1024)(128)(4,1)}), s8[4194304]{0:T(1024)(128)(4,1)S(1)}, s32[]{:S(2)}) async-start(s8[5242880]{0:T(1024)(128)(4,1)} %bitcast.28), calls=%async_computation.4 | async-start | bytes 8388608
  25.8 64.4 %slice-start.4 = ((s8[5242880]{0:T(1024)(128)(4,1)}), s8[4194304]{0:T(1024)(128)(4,1)S(1)}, s32[]{:S(2)}) async-start(s8[5242880]{0:T(1024)(128)(4,1)} %bitcast.34), calls=%async_computation.6 | async-start | bytes 8388608
  27.1 63.1 %slice-start = ((s8[5242880]{0:T(1024)(128)(4,1)}), s8[4194304]{0:T(1024)(128)(4,1)S(1)}, s32[]{:S(2)}) async-start(s8[5242880]{0:T(1024)(128)(4,1)} %bitcast.22), calls=%async_computation.2 | async-start | bytes 8388608
  27.1 63.0 %slice-start.3 = ((s8[5242880]{0:T(1024)(128)(4,1)}), s8[1048576]{0:T(1024)(128)(4,1)S(1)}, s32[]{:S(2)}) async-start(s8[5242880]{0:T(1024)(128)(4,1)} %bitcast.28), calls=%async_computation.5 | async-start | bytes 2097152
  27.1 63.0 %slice-start.5 = ((s8[5242880]{0:T(1024)(128)(4,1)}), s8[1048576]{0:T(1024)(128)(4,1)S(1)}, s32[]{:S(2)}) async-start(s8[5242880]{0:T(1024)(128)(4,1)} %bitcast.34), calls=%async_computation.7 | async-start | bytes 2097152
  89.0 1.2 slice-start.1
  89.5 5.8 %collective-permute-start.3 = (bf16[256,4096]{1,0:T(8,128)(2,1)S(1)}, bf16[256,4096]{1,0:T(8,128)(2,1)S(1)}, u32[]{:S(2)}, u32[]{:S(2)}) collective-permute-start(bf16[256,4096]{1,0:T(8,128)(2,1)S(1)} %get-tuple-element.24), channel_id=1, source_target_pairs={{0,64},{64,0},{1,65},{65,1},{2,66},{66,2},{3,67},{67,3},{4,68},{68... | collective-permute-start | bytes 6291464 | tf_op jit(solution)/shard_map/ppermute | solution.py:265
  89.6 11.3 %collective-permute-start.5 = (bf16[256,4096]{1,0:T(8,128)(2,1)S(1)}, bf16[256,4096]{1,0:T(8,128)(2,1)S(1)}, u32[]{:S(2)}, u32[]{:S(2)}) collective-permute-start(bf16[256,4096]{1,0:T(8,128)(2,1)S(1)} %get-tuple-element.23), channel_id=1, source_target_pairs={{0,64},{64,0},{1,65},{65,1},{2,66},{66,2},{3,67},{67,3},{4,68},{68... | collective-permute-start | bytes 6291464 | tf_op jit(solution)/shard_map/ppermute | solution.py:266
  100.4 6.0 %collective-permute-start.4 = (bf16[256,4096]{1,0:T(8,128)(2,1)S(1)}, bf16[256,4096]{1,0:T(8,128)(2,1)S(1)}, u32[]{:S(2)}, u32[]{:S(2)}) collective-permute-start(bf16[256,4096]{1,0:T(8,128)(2,1)S(1)} %half_expert.5), channel_id=1, source_target_pairs={{0,64},{64,0},{1,65},{65,1},{2,66},{66,2},{3,67},{67,3},{4,68},{68... | collective-permute-start | bytes 6291464 | tf_op jit(solution)/shard_map/ppermute | solution.py:269
  105.9 5.5 %collective-permute-start.6 = (bf16[256,4096]{1,0:T(8,128)(2,1)S(1)}, bf16[256,4096]{1,0:T(8,128)(2,1)S(1)}, u32[]{:S(2)}, u32[]{:S(2)}) collective-permute-start(bf16[256,4096]{1,0:T(8,128)(2,1)S(1)} %half_expert.7), channel_id=1, source_target_pairs={{0,64},{64,0},{1,65},{65,1},{2,66},{66,2},{3,67},{67,3},{4,68},{68... | collective-permute-start | bytes 6291464 | tf_op jit(solution)/shard_map/ppermute | solution.py:270

commit v4 on v3

--- a/solution.py
+++ b/solution.py
@@ -227,7 +227,7 @@
 
     own, *sent = attend_project(queries, new_kv, cache, lengths, out_weight, me, tp)
     total = own.astype(jnp.float32)
-    for hop in range(1, tp):
+    for hop in sorted(range(1, tp), key=lambda k: min(k, tp - k)):
         total = total + lax.ppermute(
             sent[hop - 1], "tp", [(i, (i + hop) % tp) for i in range(tp)]
         ).astype(jnp.float32)

time: 172 us -> 170 us (0.988)
  blocking collectives: 120 us -> 118 us
    all_to_all x1, blocking collectives: 61.9 us -> 59.7 us  [on_device(): lax.all_to_all(outgoing, ('dp', 'tp'), 0, 0, tiled=True).reshape(-1, width)]
  transfers between devices with their start and end apart: 7 -> 7, of which waited for: 2 -> 3; matrix products, arithmetic and copies ran while one was open for 2% -> 2% of each run, Pallas kernels for 12% -> 12%
where the time goes in v4:
time: 170 us
  blocking collectives  118 us (69%)
  Pallas kernels  29.7 us (17%)
  waiting for transfers between devices  8.68 us (5%)
  starting transfers between devices  7.53 us (4%)
  other arithmetic  2.22 us (1%)
  local copies, waits for them, and re-layouts  2.16 us (1%)
    all_to_all x1, blocking collectives, on_device(): lax.all_to_all(outgoing, ('dp', 'tp'), 0, 0, tiled=True).reshape(-1, width)  59.7 us
    all_to_all x1, blocking collectives, on_device(): lax.all_to_all(combined.reshape(experts, steps * slots, width), ('dp', 't...  58.6 us
    pallas_call x4, Pallas kernels, half_expert(): pl.pallas_call(functools.partial(ffn_kernel, first, count, 0 if out_rows...  20.3 us
    ppermute x3, waiting for transfers between devices, on_device(): lax.ppermute(sent[hop - 1], 'tp', [(i, (i + hop) % tp) for i in range(tp)])  8.67 us
    pallas_call x1, Pallas kernels, attend_project(): pl.pallas_call(attend_project_kernel, in_specs=[smem, smem, vmem, vmem, h...  7.88 us
    ppermute x3, starting transfers between devices, on_device(): lax.ppermute(sent[hop - 1], 'tp', [(i, (i + hop) % tp) for i in range(tp)])  6.06 us
  transfers between devices with their start and end apart: 7, of which 3 were waited for; matrix products, arithmetic and copies ran while one was open for 2% of the time, Pallas kernels for 12%

profile of v4, /device:TPU:0, one launch (start us, length us, event | category | flops | bytes accessed | tf_op | source)
XLA Modules:
  0.0 170.2 jit_solution(3606016422402973419)
XLA Ops:
  0.0 7.9 %attend_project.1 = (bf16[32,4096]{1,0:T(8,128)(2,1)}, bf16[32,4096]{1,0:T(8,128)(2,1)}, bf16[32,4096]{1,0:T(8,128)(2,1)}, bf16[32,4096]{1,0:T(8,128)(2,1)}) custom-call(s32[1]{0:T(128)} %bitcast.1.me_ref, s32[32]{0:T(128)} %lens_ref.1, bf16[4,32,1024]{2,1,0:T(8,128)(2,1)} %query_ref.1, bf16[4,2,32,128]{3,2,1,0:T(8,128)(2,1)} %new_ref.1, ...), custom_call_target="tpu_custom_call" | custom-call | tf_op jit(solution)/shard_map/attend_project/pallas_call | solution.py:130
  7.9 2.1 %collective-permute-start = (bf16[32,4096]{1,0:T(8,128)(2,1)}, bf16[32,4096]{1,0:T(8,128)(2,1)S(1)}, u32[]{:S(2)}, u32[]{:S(2)}) collective-permute-start(bf16[32,4096]{1,0:T(8,128)(2,1)} %get-tuple-element.14), channel_id=1, source_target_pairs={{0,1},{1,2},{2,3},{3,0},{4,5},{5,6},{6,7},{7,4},{8,9},{9,10},{10,1... | collective-permute-start | bytes 786440 | tf_op jit(solution)/shard_map/ppermute | solution.py:231
  10.0 2.2 %collective-permute-start.1 = (bf16[32,4096]{1,0:T(8,128)(2,1)}, bf16[32,4096]{1,0:T(8,128)(2,1)S(1)}, u32[]{:S(2)}, u32[]{:S(2)}) collective-permute-start(bf16[32,4096]{1,0:T(8,128)(2,1)} %get-tuple-element.15), channel_id=1, source_target_pairs={{0,3},{1,0},{2,1},{3,2},{4,7},{5,4},{6,5},{7,6},{8,11},{9,8},{10,9... | collective-permute-start | bytes 786440 | tf_op jit(solution)/shard_map/ppermute | solution.py:231
  12.2 1.8 %collective-permute-start.2 = (bf16[32,4096]{1,0:T(8,128)(2,1)}, bf16[32,4096]{1,0:T(8,128)(2,1)S(1)}, u32[]{:S(2)}, u32[]{:S(2)}) collective-permute-start(bf16[32,4096]{1,0:T(8,128)(2,1)} %get-tuple-element.16), channel_id=1, source_target_pairs={{0,2},{1,3},{2,0},{3,1},{4,6},{5,7},{6,4},{7,5},{8,10},{9,11},{10,... | collective-permute-start | bytes 786440 | tf_op jit(solution)/shard_map/ppermute | solution.py:231
  15.0 0.5 broadcast_and_fusion
  15.5 0.3 and.43
  16.1 0.5 broadcast_in_dim.39
  16.8 1.9 %collective-permute-done = bf16[32,4096]{1,0:T(8,128)(2,1)S(1)} collective-permute-done((bf16[32,4096]{1,0:T(8,128)(2,1)}, bf16[32,4096]{1,0:T(8,128)(2,1)S(1)}, u32[]{:S(2)}, u32[]{:S(2)}) %collective-permute-start) | collective-permute-done | bytes 262176 | tf_op jit(solution)/shard_map/ppermute | solution.py:231
  18.6 5.1 %collective-permute-done.1 = bf16[32,4096]{1,0:T(8,128)(2,1)S(1)} collective-permute-done((bf16[32,4096]{1,0:T(8,128)(2,1)}, bf16[32,4096]{1,0:T(8,128)(2,1)S(1)}, u32[]{:S(2)}, u32[]{:S(2)}) %collective-permute-start.1) | collective-permute-done | bytes 262176 | tf_op jit(solution)/shard_map/ppermute | solution.py:231
  23.7 1.7 collective-permute-done.2
  25.4 0.3 multiply_reduce_fusion
  25.8 1.3 convolution_convert_fusion
  27.1 59.7 %all_to_all.10 = bf16[64,8,4096]{2,1,0:T(8,128)(2,1)S(1)} all-to-all(bf16[64,8,4096]{2,1,0:T(8,128)(2,1)S(1)} %bitcast.44), channel_id=1, replica_groups=mesh['side'=2,'dp'=16,'tp'=4] {'dp','tp'}, dimensions={0} | all-to-all | bytes 8388608 | tf_op jit(solution)/shard_map/all_to_all | solution.py:260
  86.8 0.5 slice_bitcast_fusion
  87.3 0.5 collective-permute-start.5
  88.0 5.0 %half_expert.4 = bf16[256,4096]{1,0:T(8,128)(2,1)S(1)} custom-call(bf16[512,4096]{1,0:T(8,128)(2,1)S(1)} %bitcast.40, bf16[4096,640]{1,0:T(8,128)(2,1)S(1)} %bitcast.24, bf16[4096,640]{1,0:T(8,128)(2,1)S(1)} %bitcast.30, bf16[640,4096]{1,0:T(8,128)(2,1)S(1)} %bitcast.36), custom_call_target="tpu_custom_call" | custom-call | flops 4026531840 | bytes 4194304 | tf_op jit(solution)/shard_map/half_expert/pallas_call | solution.py:172
  93.1 5.1 %half_expert.5 = bf16[256,4096]{1,0:T(8,128)(2,1)S(1)} custom-call(bf16[256,4096]{1,0:T(8,128)(2,1)S(1)} %collective-permute-done.3.x_ref, bf16[4096,640]{1,0:T(8,128)(2,1)S(1)} %bitcast.25, bf16[4096,640]{1,0:T(8,128)(2,1)S(1)} %bitcast.31, bf16[640,4096]{1,0:T(8,128)(2,1)S(1)} %bitcast.37), custom_call_target="tpu_custom_call" | custom-call | flops 4026531840 | bytes 4194304 | tf_op jit(solution)/shard_map/half_expert/pallas_call | solution.py:172
  98.1 0.5 collective-permute-start.4
  98.6 5.0 %half_expert.7 = bf16[256,4096]{1,0:T(8,128)(2,1)S(1)} custom-call(bf16[256,4096]{1,0:T(8,128)(2,1)S(1)} %collective-permute-done.5.x_ref, bf16[4096,640]{1,0:T(8,128)(2,1)S(1)} %bitcast.26, bf16[4096,640]{1,0:T(8,128)(2,1)S(1)} %bitcast.32, bf16[640,4096]{1,0:T(8,128)(2,1)S(1)} %bitcast.38), custom_call_target="tpu_custom_call" | custom-call | flops 4026531840 | bytes 4194304 | tf_op jit(solution)/shard_map/half_expert/pallas_call | solution.py:172
  103.7 0.4 collective-permute-start.6
  104.1 5.1 %half_expert.6 = bf16[512,4096]{1,0:T(8,128)(2,1)S(1)} custom-call(bf16[512,4096]{1,0:T(8,128)(2,1)S(1)} %bitcast.41, bf16[4096,640]{1,0:T(8,128)(2,1)S(1)} %bitcast.27, bf16[4096,640]{1,0:T(8,128)(2,1)S(1)} %bitcast.33, bf16[640,4096]{1,0:T(8,128)(2,1)S(1)} %bitcast.39, bf16[256,4096]{1,0:T(8,128)(2,1)S(1)} %collective-permute-done.4.rest_0_), custom_call_target="tpu_custom_call" | custom-call | flops 4026531840 | bytes 4194304 | tf_op jit(solution)/shard_map/half_expert/pallas_call | solution.py:172
  109.2 0.8 fusion
  110.0 58.6 %all_to_all.11 = bf16[64,8,4096]{2,1,0:T(8,128)(2,1)S(1)} all-to-all(bf16[64,8,4096]{2,1,0:T(8,128)(2,1)S(1)} %bitcast.42), channel_id=1, replica_groups=mesh['side'=2,'dp'=16,'tp'=4] {'dp','tp'}, dimensions={0} | all-to-all | bytes 8388608 | tf_op jit(solution)/shard_map/all_to_all | solution.py:274
  168.6 1.6 mix.1
  (49 shorter events, 1.6 us)
Async XLA Ops:
  0.0 14.0 %copy-start.2 = (s32[4,8,8]{2,1,0:T(8,128)S(1)}, s32[4,8,8]{2,1,0:T(8,128)}, u32[]{:S(2)}) copy-start(s32[4,8,8]{2,1,0:T(8,128)} %param.19) | copy-start | bytes 3076
  0.0 14.3 %copy-start.4 = (bf16[4096]{0:T(1024)(128)(2,1)S(1)}, bf16[4096]{0:T(1024)(128)(2,1)}, u32[]{:S(2)}) copy-start(bf16[4096]{0:T(1024)(128)(2,1)} %param.18) | copy-start | bytes 24580
  0.0 14.3 %copy-start.3 = (f32[4,8,8]{2,1,0:T(8,128)S(1)}, f32[4,8,8]{2,1,0:T(8,128)}, u32[]{:S(2)}) copy-start(f32[4,8,8]{2,1,0:T(8,128)} %param.20) | copy-start | bytes 3076
  7.9 17.5 %copy-start = (bf16[4,8,4096]{2,1,0:T(8,128)(2,1)S(1)}, bf16[4,8,4096]{2,1,0:T(8,128)(2,1)}, u32[]{:S(2)}) copy-start(bf16[4,8,4096]{2,1,0:T(8,128)(2,1)} %param.12) | copy-start | bytes 786436
  7.9 17.5 %copy-start.1 = (bf16[32,4096]{1,0:T(8,128)(2,1)S(1)}, bf16[32,4096]{1,0:T(8,128)(2,1)}, u32[]{:S(2)}) copy-start(bf16[32,4096]{1,0:T(8,128)(2,1)} %get-tuple-element.13) | copy-start | bytes 786436
  7.9 10.7 %collective-permute-start = (bf16[32,4096]{1,0:T(8,128)(2,1)}, bf16[32,4096]{1,0:T(8,128)(2,1)S(1)}, u32[]{:S(2)}, u32[]{:S(2)}) collective-permute-start(bf16[32,4096]{1,0:T(8,128)(2,1)} %get-tuple-element.14), channel_id=1, source_target_pairs={{0,1},{1,2},{2,3},{3,0},{4,5},{5,6},{6,7},{7,4},{8,9},{9,10},{10,1... | collective-permute-start | bytes 786440 | tf_op jit(solution)/shard_map/ppermute | solution.py:231
  10.0 13.7 %collective-permute-start.1 = (bf16[32,4096]{1,0:T(8,128)(2,1)}, bf16[32,4096]{1,0:T(8,128)(2,1)S(1)}, u32[]{:S(2)}, u32[]{:S(2)}) collective-permute-start(bf16[32,4096]{1,0:T(8,128)(2,1)} %get-tuple-element.15), channel_id=1, source_target_pairs={{0,3},{1,0},{2,1},{3,2},{4,7},{5,4},{6,5},{7,6},{8,11},{9,8},{10,9... | collective-permute-start | bytes 786440 | tf_op jit(solution)/shard_map/ppermute | solution.py:231
  12.2 13.2 %collective-permute-start.2 = (bf16[32,4096]{1,0:T(8,128)(2,1)}, bf16[32,4096]{1,0:T(8,128)(2,1)S(1)}, u32[]{:S(2)}, u32[]{:S(2)}) collective-permute-start(bf16[32,4096]{1,0:T(8,128)(2,1)} %get-tuple-element.16), channel_id=1, source_target_pairs={{0,2},{1,3},{2,0},{3,1},{4,6},{5,7},{6,4},{7,5},{8,10},{9,11},{10,... | collective-permute-start | bytes 786440 | tf_op jit(solution)/shard_map/ppermute | solution.py:231
  25.7 62.1 %slice-start.2 = ((s8[5242880]{0:T(1024)(128)(4,1)}), s8[4194304]{0:T(1024)(128)(4,1)S(1)}, s32[]{:S(2)}) async-start(s8[5242880]{0:T(1024)(128)(4,1)} %bitcast.28), calls=%async_computation.4 | async-start | bytes 8388608
  25.8 62.1 %slice-start.4 = ((s8[5242880]{0:T(1024)(128)(4,1)}), s8[4194304]{0:T(1024)(128)(4,1)S(1)}, s32[]{:S(2)}) async-start(s8[5242880]{0:T(1024)(128)(4,1)} %bitcast.34), calls=%async_computation.6 | async-start | bytes 8388608
  27.1 60.8 %slice-start = ((s8[5242880]{0:T(1024)(128)(4,1)}), s8[4194304]{0:T(1024)(128)(4,1)S(1)}, s32[]{:S(2)}) async-start(s8[5242880]{0:T(1024)(128)(4,1)} %bitcast.22), calls=%async_computation.2 | async-start | bytes 8388608
  27.1 60.8 %slice-start.3 = ((s8[5242880]{0:T(1024)(128)(4,1)}), s8[1048576]{0:T(1024)(128)(4,1)S(1)}, s32[]{:S(2)}) async-start(s8[5242880]{0:T(1024)(128)(4,1)} %bitcast.28), calls=%async_computation.5 | async-start | bytes 2097152
  27.1 60.8 %slice-start.5 = ((s8[5242880]{0:T(1024)(128)(4,1)}), s8[1048576]{0:T(1024)(128)(4,1)S(1)}, s32[]{:S(2)}) async-start(s8[5242880]{0:T(1024)(128)(4,1)} %bitcast.34), calls=%async_computation.7 | async-start | bytes 2097152
  86.8 1.2 slice-start.1
  87.3 5.8 %collective-permute-start.3 = (bf16[256,4096]{1,0:T(8,128)(2,1)S(1)}, bf16[256,4096]{1,0:T(8,128)(2,1)S(1)}, u32[]{:S(2)}, u32[]{:S(2)}) collective-permute-start(bf16[256,4096]{1,0:T(8,128)(2,1)S(1)} %get-tuple-element.24), channel_id=1, source_target_pairs={{0,64},{64,0},{1,65},{65,1},{2,66},{66,2},{3,67},{67,3},{4,68},{68... | collective-permute-start | bytes 6291464 | tf_op jit(solution)/shard_map/ppermute | solution.py:265
  87.3 11.3 %collective-permute-start.5 = (bf16[256,4096]{1,0:T(8,128)(2,1)S(1)}, bf16[256,4096]{1,0:T(8,128)(2,1)S(1)}, u32[]{:S(2)}, u32[]{:S(2)}) collective-permute-start(bf16[256,4096]{1,0:T(8,128)(2,1)S(1)} %get-tuple-element.23), channel_id=1, source_target_pairs={{0,64},{64,0},{1,65},{65,1},{2,66},{66,2},{3,67},{67,3},{4,68},{68... | collective-permute-start | bytes 6291464 | tf_op jit(solution)/shard_map/ppermute | solution.py:266
  98.1 6.0 %collective-permute-start.4 = (bf16[256,4096]{1,0:T(8,128)(2,1)S(1)}, bf16[256,4096]{1,0:T(8,128)(2,1)S(1)}, u32[]{:S(2)}, u32[]{:S(2)}) collective-permute-start(bf16[256,4096]{1,0:T(8,128)(2,1)S(1)} %half_expert.5), channel_id=1, source_target_pairs={{0,64},{64,0},{1,65},{65,1},{2,66},{66,2},{3,67},{67,3},{4,68},{68... | collective-permute-start | bytes 6291464 | tf_op jit(solution)/shard_map/ppermute | solution.py:269
  103.7 5.5 %collective-permute-start.6 = (bf16[256,4096]{1,0:T(8,128)(2,1)S(1)}, bf16[256,4096]{1,0:T(8,128)(2,1)S(1)}, u32[]{:S(2)}, u32[]{:S(2)}) collective-permute-start(bf16[256,4096]{1,0:T(8,128)(2,1)S(1)} %half_expert.7), channel_id=1, source_target_pairs={{0,64},{64,0},{1,65},{65,1},{2,66},{66,2},{3,67},{67,3},{4,68},{68... | collective-permute-start | bytes 6291464 | tf_op jit(solution)/shard_map/ppermute | solution.py:270
